TPU v7x, 32 devices: a whole 2x2x4 slice. The times are simulated.
32 devices in a mesh: segment: 2 (over core), seq: 16 (over z, y, x).
Axes of the slice: x: 2, y: 2, z: 4, core: 2. Of those that a mesh axis runs over, the one named last changes fastest.
Arguments:
- tracks_in: bfloat16 [1, 16, 512, 1536], P(None, 'seq'), may hold values from -120 to 120
- w_qkv: bfloat16 [2, 1536, 2304], P('segment'), may hold values from -0.15625 to 0.15625
- w_out: bfloat16 [2, 768, 1536], P('segment'), may hold values from -0.21875 to 0.21875
- visible: int32 [1, 16, 512], P(None, 'seq'), may hold values 0 or 1
- neighbours: int32 [1, 1, 4, 2], replicated, may hold values from 0 to 3, as said below
Outputs:
- section_tokens: bfloat16 [2, 1, 16, 512, 1536], P('segment', None, 'seq')
Inputs may be any that keep to these rules, and one draw needn't show every extreme that they name: `neighbours`: each row names 2 different track blocks, none of them the row's own block.
All inputs are finite; a program needn't handle non-finite values. No bound on the sum of `visible` on one device may be relied on, other than what follows from the above.
Results may differ from a plain program's by a relative error of at most 0.0042.
Values may be sent and summed in bfloat16 or wider, within the bound.
A program may use at most 128 MiB of HBM per device.

v0:
```python
import math

import jax
import jax.numpy as jnp
from jax import lax
from jax.sharding import PartitionSpec as P

HEADS = 6
HDIM = 128
BLOCK = 128
NB = 2
FRAMES = 16


epsilon = 1e-06


def partner(shard, axis, distance):
    return lax.ppermute(shard, axis, [(i, i ^ 1 << distance) for i in range(lax.axis_size(axis))])


def from_behind(value, axis, steps):
    count = lax.axis_size(axis)
    initial, last = (max(0, -steps), min(count, count - steps))
    return lax.ppermute(value, axis, [(source, source + steps) for source in range(initial, last)])


def normalize(tokens):
    widened = tokens.astype(jnp.float32)
    factor = lax.rsqrt(jnp.mean(widened * widened, axis=-1, keepdims=True) + epsilon)
    return (widened * factor).astype(jnp.bfloat16)


def project(tokens, weight):
    return jnp.dot(normalize(tokens), weight, preferred_element_type=jnp.float32).astype(
        jnp.bfloat16
    )


def finish(tokens, mixed_heads, weight):
    delta_rows = jnp.dot(mixed_heads, weight, preferred_element_type=jnp.float32)
    return (tokens.astype(jnp.float32) + delta_rows).astype(jnp.bfloat16)


def time_branch(projected, count, seq_size):
    inner = HEADS * HDIM
    shaped = projected.reshape(seq_size // FRAMES, FRAMES, count, 3, HEADS, HDIM)
    scores = jnp.einsum(
        "vfphd,vgphd->vphfg",
        shaped[:, :, :, 0],
        shaped[:, :, :, 1],
        preferred_element_type=jnp.float32,
    ) / math.sqrt(HDIM)
    exponent = jnp.exp(scores)
    weights = (exponent / jnp.sum(exponent, axis=-1, keepdims=True)).astype(jnp.bfloat16)
    mixed_heads = jnp.einsum(
        "vphfg,vgphd->vfphd", weights, shaped[:, :, :, 2], preferred_element_type=jnp.float32
    )
    return mixed_heads.reshape(-1, inner).astype(jnp.bfloat16)


def track_branch(projected, seen_mask, chosen, start_block, count):
    inner = HEADS * HDIM
    blocks_count = projected.shape[0] // BLOCK
    blocks_all = projected.reshape(blocks_count, BLOCK, 3, HEADS, HDIM)
    own_block = lax.broadcasted_iota(jnp.int32, (count, 1), 0) + start_block
    listing = jnp.concatenate(
        [own_block, lax.dynamic_slice_in_dim(chosen, start_block, count, 0)], axis=1
    )
    queries = lax.dynamic_slice_in_dim(blocks_all[:, :, 0], start_block, count, 0)
    keys_sel = jnp.take(blocks_all[:, :, 1], listing, axis=0)
    values_sel = jnp.take(blocks_all[:, :, 2], listing, axis=0)
    seen_sel = jnp.take(seen_mask.reshape(blocks_count, BLOCK), listing, axis=0)
    scores = jnp.einsum(
        "bqhd,bjkhd->bhqjk", queries, keys_sel, preferred_element_type=jnp.float32
    ) / math.sqrt(HDIM)
    shape_mask = (BLOCK, NB + 1, BLOCK)
    itself = (lax.broadcasted_iota(jnp.int32, shape_mask, 1) == 0) & (
        lax.broadcasted_iota(jnp.int32, shape_mask, 0)
        == lax.broadcasted_iota(jnp.int32, shape_mask, 2)
    )
    allowed = (seen_sel[:, None, None, :, :] == 1) | itself[None, None]
    exponent = jnp.where(allowed, jnp.exp(scores), jnp.zeros_like(scores))
    totals = jnp.sum(exponent, axis=(-2, -1), keepdims=True)
    weights = (exponent / totals).astype(jnp.bfloat16)
    mixed_heads = jnp.einsum(
        "bhqjk,bjkhd->bqhd", weights, values_sel, preferred_element_type=jnp.float32
    )
    return mixed_heads.reshape(count * BLOCK, inner).astype(jnp.bfloat16)


def on_device(tracks_in, w_qkv, w_out, visible, neighbours):
    segment_no = lax.axis_index("segment")
    seq_no = lax.axis_index("seq")
    seq_size = lax.axis_size("seq")
    segment_size = lax.axis_size("segment")
    tracks = tracks_in.shape[2]
    width = tracks_in.shape[3]
    per_device = tracks // seq_size
    blocks_count = tracks // BLOCK
    video_no = seq_no // FRAMES
    w_both, out_both = (
        lax.all_gather(w_qkv, "segment", axis=0, tiled=True),
        lax.all_gather(w_out, "segment", axis=0, tiled=True),
    )
    half = per_device // segment_size
    query_blocks = blocks_count // segment_size
    start_block = segment_no * query_blocks
    pieces = tracks_in[0, 0].reshape(seq_size, per_device, width)
    mine = lax.dynamic_slice_in_dim(pieces, segment_no * half, half, 1)
    moved = lax.all_to_all(mine, "seq", split_axis=0, concat_axis=0, tiled=True)
    flat = moved.reshape(seq_size * half, width)
    mixed_time = time_branch(project(flat, w_both[0]), half, seq_size)
    first_half = finish(flat, mixed_time, out_both[0]).reshape(seq_size, half, width)
    other_half = partner(first_half, "segment", 0)
    full_first = jnp.where(
        segment_no == 0,
        jnp.concatenate([first_half, other_half], axis=1),
        jnp.concatenate([other_half, first_half], axis=1),
    )
    frame_rows = lax.all_to_all(full_first, "seq", split_axis=0, concat_axis=0, tiled=True).reshape(
        tracks, width
    )
    projected = project(frame_rows, w_both[1])
    lists_now = lax.dynamic_index_in_dim(neighbours[0], video_no, 0, keepdims=False)
    mixed_track = track_branch(projected, visible[0, 0], lists_now, start_block, query_blocks)
    own_rows = lax.dynamic_slice_in_dim(frame_rows, start_block * BLOCK, query_blocks * BLOCK, 0)
    second_part = finish(own_rows, mixed_track, out_both[1])
    lower_part = from_behind(second_part, "segment", 1)
    full_second = jnp.concatenate([lower_part, second_part], axis=0)
    finals = [jnp.where(segment_no == 0, full_first.reshape(tracks, width), full_second)]
    return jnp.stack(finals)[None, :, None]


def solution(mesh):
    return jax.shard_map(
        on_device,
        mesh=mesh,
        in_specs=(
            P(None, "seq", None, None),
            P("segment", None, None),
            P("segment", None, None),
            P(None, "seq", None),
            P(),
        ),
        out_specs=P("segment", None, "seq", None, None),
        check_vma=False,
    )
```

profile of v0, /device:TPU:9, one launch (start us, length us, event | category | flops | bytes accessed | tf_op | source)
XLA Modules:
  0.0 153.4 jit_solution(18281858345742629384)
XLA Ops:
  6.5 0.7 all-gather.3.cloned.1.call-update
  7.3 0.7 all-gather.5.cloned.1.call-update
  8.1 26.0 %all_to_all.10 = bf16[16,16,1536]{2,1,0:T(8,128)(2,1)S(1)} all-to-all(bf16[16,16,1536]{2,1,0:T(8,128)(2,1)S(1)} %constant_dynamic-slice_fusion.2), channel_id=1, replica_groups=mesh['segment'=2,'seq'=16] {'seq'}, dimensions={0} | all-to-all | bytes 1572864 | tf_op jit(solution)/shard_map/all_to_all | solution.py:111
  34.1 0.2 multiply_reduce_fusion
  34.4 0.2 multiply_convert_fusion
  34.6 2.7 %all-gather.3.cloned.1.call-done = bf16[2,1536,2304]{2,1,0:T(8,128)(2,1)} async-done(((bf16[1,1536,2304]{2,1,0:T(8,128)(2,1)}), bf16[2,1536,2304]{2,1,0:T(8,128)(2,1)}) %all-gather.3.cloned.1.call-update) | async-done | bytes 14155792 | tf_op jit(solution)/shard_map/all_gather | solution.py:103
  37.3 6.0 %fusion.3 = bf16[256,2304]{1,0:T(8,128)(2,1)} fusion(bf16[256,1536]{1,0:T(8,128)(2,1)S(1)} %bitcast.101, bf16[2,1536,2304]{2,1,0:T(8,128)(2,1)} %all-gather.3.cloned.1.call-done), kind=kOutput, calls=%fused_computation.10 | convolution fusion | flops 1812529152 | bytes 9043968 | tf_op jit(solution)/shard_map/dot_general | solution.py:35
  43.3 2.9 %reshape.246 = bf16[1,16,16,3,6,128]{5,4,3,2,1,0:T(8,128)(2,1)S(1)} reshape(bf16[256,2304]{1,0:T(8,128)(2,1)} %fusion.3) | data formatting | bytes 2359296 | tf_op jit(solution)/shard_map/reshape | solution.py:47
  46.2 1.1 fusion.31
  47.3 0.6 fusion.9
  47.9 0.5 copy-done.6
  48.4 0.5 fusion.11
  48.8 0.1 copy.51
  49.0 5.5 %all-gather.5.cloned.1.call-done = bf16[2,768,1536]{2,1,0:T(8,128)(2,1)} async-done(((bf16[1,768,1536]{2,1,0:T(8,128)(2,1)}), bf16[2,768,1536]{2,1,0:T(8,128)(2,1)}) %all-gather.5.cloned.1.call-update) | async-done | bytes 4718608 | tf_op jit(solution)/shard_map/all_gather | solution.py:104
  54.5 2.4 %fusion.6 = bf16[256,1536]{1,0:T(8,128)(2,1)S(1)} fusion(bf16[2,768,1536]{2,1,0:T(8,128)(2,1)} %all-gather.5.cloned.1.call-done, bf16[32,8,6,128]{3,2,1,0:T(8,128)(2,1)S(1)} %bitcast.104, bf16[256,1536]{1,0:T(8,128)(2,1)S(1)} %bitcast.92), kind=kOutput, calls=%fused_computation.15 | convolution fusion | flops 605159424 | bytes 4325376 | tf_op jit(solution)/shard_map/dot_general | solution.py:41
  56.9 0.3 collective-permute-start
  57.2 2.1 %collective-permute-done = bf16[16,16,1536]{2,1,0:T(8,128)(2,1)S(1)} collective-permute-done((bf16[16,16,1536]{2,1,0:T(8,128)(2,1)S(1)}, bf16[16,16,1536]{2,1,0:T(8,128)(2,1)S(1)}, u32[]{:S(2)}, u32[]{:S(2)}) %collective-permute-start) | collective-permute-done | bytes 786464 | tf_op jit(solution)/shard_map/ppermute | solution.py:19
  59.3 1.8 %maximum_select_fusion = bf16[16,32,1536]{2,1,0:T(8,128)(2,1)} fusion(bf16[16,16,1536]{2,1,0:T(8,128)(2,1)S(1)} %collective-permute-done, bf16[16,16,1536]{2,1,0:T(8,128)(2,1)S(1)} %bitcast.103, pred[]{:T(512)S(6)} %eq.29), kind=kLoop, calls=%fused_computation.22 | loop fusion | flops 7077888 | bytes 3145729 | tf_op jit(solution)/shard_map/jit(_where)/select_n | solution.py:116
  61.1 6.5 %all-to-all-start.1 = ((bf16[16,32,1536]{2,1,0:T(8,128)(2,1)}), bf16[16,32,1536]{2,1,0:T(8,128)(2,1)S(1)}, u32[]{:S(2)}, u32[]{:S(2)}) async-start(bf16[16,32,1536]{2,1,0:T(8,128)(2,1)} %maximum_select_fusion), calls=%async_computation.1 | async-start | bytes 3145728 | tf_op jit(solution)/shard_map/all_to_all | solution.py:121
  67.7 0.1 copy.52
  68.2 0.6 gather_fusion
  68.9 0.8 broadcast_or_fusion
  69.7 33.5 %all-to-all-done.1 = bf16[16,32,1536]{2,1,0:T(8,128)(2,1)S(1)} async-done(((bf16[16,32,1536]{2,1,0:T(8,128)(2,1)}), bf16[16,32,1536]{2,1,0:T(8,128)(2,1)S(1)}, u32[]{:S(2)}, u32[]{:S(2)}) %all-to-all-start.1) | async-done | bytes 1572896 | tf_op jit(solution)/shard_map/all_to_all | solution.py:121
  103.3 0.4 fusion.4
  103.6 0.3 fusion.5
  104.0 8.0 %fusion.2 = bf16[512,2304]{1,0:T(8,128)(2,1)} fusion(bf16[512,1536]{1,0:T(8,128)(2,1)S(1)} %bitcast.98, bf16[2,1536,2304]{2,1,0:T(8,128)(2,1)} %all-gather.3.cloned.1.call-done), kind=kOutput, calls=%fused_computation.7 | convolution fusion | flops 3625058304 | bytes 11010048 | tf_op jit(solution)/shard_map/dot_general | solution.py:35
  112.0 4.3 %copy.53 = bf16[512,2304]{0,1:T(8,128)(2,1)} copy(bf16[512,2304]{1,0:T(8,128)(2,1)} %fusion.2) | data formatting | bytes 4718592 | tf_op jit(solution)/shard_map/convert_element_type | solution.py:35
  116.3 5.3 %reshape.252 = bf16[4,128,3,6,128]{1,0,4,3,2:T(4,128)(2,1)} reshape(bf16[512,2304]{0,1:T(8,128)(2,1)} %copy.53) | data formatting | bytes 4718592 | tf_op jit(solution)/shard_map/reshape | solution.py:65
  121.6 3.7 %fusion.30 = (bf16[4,128,1,6,128]{1,0,4,3,2:T(4,128)(2,1)}, bf16[4,128,1,6,128]{1,0,4,3,2:T(4,128)(2,1)S(1)}, bf16[4,128,1,6,128]{1,0,4,3,2:T(4,128)(2,1)}) fusion(bf16[4,128,3,6,128]{1,0,4,3,2:T(4,128)(2,1)} %reshape.252), kind=kLoop, calls=%fused_computation.70 | loop fusion | bytes 4718592 | tf_op jit(solution)/shard_map/slice | solution.py:70
  125.3 0.6 copy.71
  125.9 1.6 %copy.72 = bf16[4,128,1,6,128]{4,1,3,0,2:T(8,128)(2,1)S(1)} copy(bf16[4,128,1,6,128]{1,0,4,3,2:T(4,128)(2,1)} %get-tuple-element.10) | data formatting | bytes 1572864
  127.5 1.8 %gather_fusion.1 = bf16[6,128,6,128]{3,1,2,0:T(8,128)(2,1)} fusion(bf16[4,128,6,128]{3,1,2,0:T(8,128)(2,1)S(1)} %bitcast.94, s32[1024]{0:T(1024)S(1)} %pad_clamp_fusion.1), kind=kCustom, calls=%fused_computation.clone | custom fusion | bytes 2359320 | tf_op jit(solution)/shard_map/jit(_take)/gather | solution.py:72
  129.3 1.8 %gather_fusion.2 = bf16[6,128,6,128]{3,1,2,0:T(8,128)(2,1)} fusion(bf16[4,128,6,128]{3,1,2,0:T(8,128)(2,1)S(1)} %bitcast.93, s32[1024]{0:T(1024)S(1)} %pad_clamp_fusion.1), kind=kCustom, calls=%fused_computation.1.clone | custom fusion | bytes 2359320 | tf_op jit(solution)/shard_map/jit(_take)/gather | solution.py:71
  131.0 2.6 %broadcast_select_fusion = (bf16[2,3,128,6,128]{4,2,3,1,0:T(8,128)(2,1)S(1)}, bf16[2,3,128,6,128]{4,2,3,1,0:T(8,128)(2,1)}) fusion(bf16[2,3,128,6,128]{4,2,3,1,0:T(8,128)(2,1)} %bitcast.96, pred[2,3]{1,0:T(4,128)(4,1)S(1)} %get-tuple-element.6, bf16[2,3,128,6,128]{4,2,3,1,0:T(8,128)(2,1)S(1)} %bitcast.95), kind=kLoop, calls=%fused_computation.34 | loop fusion | flops 1179648 | bytes 4718598 | tf_op jit(solution)/shard_map/jit(_take)/select_n | solution.py:71
  133.7 1.0 copy-done.3
  134.7 0.4 constant_dynamic-slice_fusion
  135.1 0.4 copy.57
  135.6 0.5 fusion.19
  136.1 0.4 copy-done.7
  136.5 0.4 fusion.8
  136.9 0.4 copy-done.4
  137.3 1.0 fusion.12
  138.3 0.4 copy.62
  138.8 0.2 slice-done.1
  138.9 0.8 fusion.7
  139.7 1.3 collective-permute-start.1
  141.0 4.0 %collective-permute-done.1 = bf16[256,1536]{1,0:T(8,128)(2,1)S(1)} collective-permute-done((bf16[256,1536]{1,0:T(8,128)(2,1)S(1)}, bf16[256,1536]{1,0:T(8,128)(2,1)S(1)}, u32[]{:S(2)}, u32[]{:S(2)}) %collective-permute-start.1) | collective-permute-done | bytes 786464 | tf_op jit(solution)/shard_map/ppermute | solution.py:25
  145.1 1.5 %maximum_select_fusion.1 = bf16[1,1,1,512,1536]{4,3,2,1,0:T(8,128)(2,1)} fusion(bf16[1,1,1,512,1536]{4,3,2,1,0:T(8,128)(2,1)} %bitcast.11, bf16[1,1,1,256,1536]{4,3,2,1,0:T(8,128)(2,1)S(1)} %bitcast.99, bf16[1,1,1,256,1536]{4,3,2,1,0:T(8,128)(2,1)S(1)} %bitcast.100, pred[]{:T(512)S(6)} %eq.29), kind=kLoop, calls=%fused_computation.23 | loop fusion | flops 3932160 | bytes 4718593 | tf_op jit(solution)/shard_map/jit(_where)/select_n | solution.py:131
  (37 shorter events, 0.9 us)
Async XLA Ops:
  6.5 1.5 copy-start
  6.5 30.8 %all-gather.3.cloned.1.call-start = ((), (), s32[]{:S(2)}) async-start(), calls=%async_computation.2 | async-start | bytes 21233664 | tf_op jit(solution)/shard_map/all_gather | solution.py:103
  7.3 47.2 %all-gather.5.cloned.1.call-start = ((), (), s32[]{:S(2)}) async-start(), calls=%async_computation.3 | async-start | bytes 7077888 | tf_op jit(solution)/shard_map/all_gather | solution.py:104
  47.3 1.1 copy-start.6
  56.9 2.4 %collective-permute-start = (bf16[16,16,1536]{2,1,0:T(8,128)(2,1)S(1)}, bf16[16,16,1536]{2,1,0:T(8,128)(2,1)S(1)}, u32[]{:S(2)}, u32[]{:S(2)}) collective-permute-start(bf16[16,16,1536]{2,1,0:T(8,128)(2,1)S(1)} %bitcast.102), channel_id=1, source_target_pairs={{0,16},{16,0},{1,17},{17,1},{2,18},{18,2},{3,19},{19,3},{4,20},{20... | collective-permute-start | bytes 2359304 | tf_op jit(solution)/shard_map/ppermute | solution.py:19
  61.1 6.6 %copy-start.8 = (s32[1,1,4,2]{2,3,1,0:T(2,128)S(1)}, s32[1,1,4,2]{2,3,1,0:T(2,128)}, u32[]{:S(2)}) copy-start(s32[1,1,4,2]{2,3,1,0:T(2,128)} %param.11) | copy-start | bytes 100
  61.1 7.1 %copy-start.5 = (s32[1,1,512]{2,1,0:T(1,128)S(1)}, s32[1,1,512]{2,1,0:T(1,128)}, u32[]{:S(2)}) copy-start(s32[1,1,512]{2,1,0:T(1,128)} %param.10) | copy-start | bytes 6148
  61.1 42.2 %all-to-all-start.1 = ((bf16[16,32,1536]{2,1,0:T(8,128)(2,1)}), bf16[16,32,1536]{2,1,0:T(8,128)(2,1)S(1)}, u32[]{:S(2)}, u32[]{:S(2)}) async-start(bf16[16,32,1536]{2,1,0:T(8,128)(2,1)} %maximum_select_fusion), calls=%async_computation.1 | async-start | bytes 3145728 | tf_op jit(solution)/shard_map/all_to_all | solution.py:121
  129.3 1.8 %copy-start.2 = (bf16[6,128,6,128]{3,1,2,0:T(8,128)(2,1)S(1)}, bf16[6,128,6,128]{3,1,2,0:T(8,128)(2,1)}, u32[]{:S(2)}) copy-start(bf16[6,128,6,128]{3,1,2,0:T(8,128)(2,1)} %gather_fusion.1) | copy-start | bytes 3538948
  133.6 1.1 copy-start.3
  135.6 0.9 copy-start.7
  136.1 1.3 copy-start.4
  136.5 2.3 %slice-start = ((s8[4718592]{0:T(1024)(128)(4,1)}), s8[4194304]{0:T(1024)(128)(4,1)S(1)}, s32[]{:S(2)}) async-start(s8[4718592]{0:T(1024)(128)(4,1)} %bitcast.109), calls=%async_computation.4 | async-start | bytes 8388608
  137.3 1.6 %slice-start.1 = ((s8[4718592]{0:T(1024)(128)(4,1)}), s8[524288]{0:T(1024)(128)(4,1)S(1)}, s32[]{:S(2)}) async-start(s8[4718592]{0:T(1024)(128)(4,1)} %bitcast.109), calls=%async_computation.5 | async-start | bytes 1048576
  139.7 5.3 %collective-permute-start.1 = (bf16[256,1536]{1,0:T(8,128)(2,1)S(1)}, bf16[256,1536]{1,0:T(8,128)(2,1)S(1)}, u32[]{:S(2)}, u32[]{:S(2)}) collective-permute-start(bf16[256,1536]{1,0:T(8,128)(2,1)S(1)} %fusion.7), channel_id=1, source_target_pairs={{0,16},{1,17},{2,18},{3,19},{4,20},{5,21},{6,22},{7,23},{8,24},{9,... | collective-permute-start | bytes 2359304 | tf_op jit(solution)/shard_map/ppermute | solution.py:25
  145.0 1.6 %copy-start.1 = (bf16[1,1,512,1536]{3,2,1,0:T(8,128)(2,1)S(1)}, bf16[1,1,512,1536]{3,2,1,0:T(8,128)(2,1)}, u32[]{:S(2)}) copy-start(bf16[1,1,512,1536]{3,2,1,0:T(8,128)(2,1)} %param.7) | copy-start | bytes 4718596
Sparse Core Ops, SparseCore 0:
  8.9 28.3 all-gather.2
  38.8 15.5 all-gather.4
where the time goes:
time: 155 us; the launch traced here: 153 us
  waiting for transfers between devices  49.2 us (32%)
  local copies, waits for them, and re-layouts  28 us (18%)
  blocking collectives  26 us (17%)
  matrix products  19.8 us (13%)
  between operations  13.6 us (9%)
  other arithmetic  8.69 us (6%)
  starting transfers between devices  8.15 us (5%)
    all_to_all x1, waiting for transfers between devices, on_device(): lax.all_to_all(full_first, 'seq', split_axis=0, concat_axis=0, tiled=True)  33.5 us
    all_to_all x1, blocking collectives, on_device(): moved = lax.all_to_all(mine, 'seq', split_axis=0, concat_axis=0, tiled=True)  26 us
    dot_general x2, matrix products, project(): jnp.dot(normalize(tokens), weight, preferred_element_type=jnp.float32)  14 us
    all_to_all x1, starting transfers between devices, on_device(): lax.all_to_all(full_first, 'seq', split_axis=0, concat_axis=0, tiled=True)  6.54 us
    all_gather x1, waiting for transfers between devices, on_device(): lax.all_gather(w_out, 'segment', axis=0, tiled=True)  5.47 us
    reshape x1, local copies, waits for them, and re-layouts, track_branch(): blocks_all = projected.reshape(blocks_count, BLOCK, 3, HEADS, HDIM)  5.28 us
    unnamed x24, local copies, waits for them, and re-layouts  4.81 us
    convert_element_type x1, local copies, waits for them, and re-layouts, project(): jnp.dot(normalize(tokens), weight, preferred_element_type=jnp.float32)  4.28 us
  transfers between devices with their start and end apart: 5, of which 5 were waited for; matrix products, arithmetic and copies ran while one was open for 9% of the time, Pallas kernels for 0%

commit v1 on v0

--- a/solution.py
+++ b/solution.py
@@ -1,8 +1,11 @@
+import functools
 import math
 
 import jax
 import jax.numpy as jnp
 from jax import lax
+from jax.experimental import pallas as pl
+from jax.experimental.pallas import tpu as pltpu
 from jax.sharding import PartitionSpec as P
 
 HEADS = 6
@@ -132,9 +135,451 @@
     return jnp.stack(finals)[None, :, None]
 
 
+INNER = HEADS * HDIM
+HALF_HEADS = HEADS // 2
+HALF_INNER = HALF_HEADS * HDIM
+MESH = pl.DeviceIdType.MESH
+SCALE_LOG2 = math.log2(math.e) / math.sqrt(HDIM)
+
+
+def dot(a, b):
+    return jnp.dot(a, b, preferred_element_type=jnp.float32)
+
+
+def dot_t(a, b):
+    return lax.dot_general(a, b, (((1,), (1,)), ((), ())), preferred_element_type=jnp.float32)
+
+
+def fused_kernel(
+    n,
+    half,
+    x_ref,
+    wq_ref,
+    wo_ref,
+    seen_ref,
+    near_ref,
+    out_ref,
+    wq0,
+    wo0,
+    wq1,
+    wo1,
+    x_got,
+    x_norm,
+    x_frame,
+    qkv0,
+    mix0,
+    first0,
+    mix_frame,
+    first1,
+    qkv1,
+    mix1,
+    mix1_low,
+    second,
+    w_sem,
+    w_send,
+    x_send,
+    x_recv,
+    frame_sem,
+    m_send,
+    m_recv,
+    f_send,
+    f_recv,
+    low_send,
+    low_recv,
+    out_sem,
+    out_send,
+    out_recv,
+):
+    s = lax.axis_index("segment")
+    me = lax.axis_index("seq")
+    sibling = {"segment": 1 - s, "seq": me}
+    group = 2 * half
+    tokens = n * half
+    tracks = n * group
+    blocks = tracks // BLOCK
+
+    def peer(d):
+        return {"segment": s, "seq": d}
+
+    barrier = pltpu.get_barrier_semaphore()
+
+    def greet(k, c):
+        pl.semaphore_signal(
+            barrier, inc=1, device_id=peer(lax.rem(me + k, n)), device_id_type=MESH
+        )
+        return c
+
+    lax.fori_loop(1, n, greet, 0)
+    pl.semaphore_signal(barrier, inc=1, device_id=sibling, device_id_type=MESH)
+
+    def rows(index, size):
+        return pl.ds(pl.multiple_of(index * size, size), size)
+
+    def x_copy(d, source):
+        return pltpu.make_async_remote_copy(
+            src_ref=x_ref.at[rows(2 * d + s, half), :],
+            dst_ref=x_got.at[rows(source, half), :],
+            send_sem=x_send.at[d],
+            recv_sem=x_recv.at[source],
+            device_id=peer(d),
+            device_id_type=MESH,
+        )
+
+    def wq1_cols(core, j):
+        return pl.ds(pl.multiple_of(j * INNER + core * HALF_INNER, HDIM), HALF_INNER)
+
+    def wq1_dst(j):
+        return wq1.at[:, pl.ds(j * HALF_INNER, HALF_INNER)]
+
+    own_x = pltpu.make_async_copy(
+        x_ref.at[rows(2 * me + s, half), :], x_got.at[rows(me, half), :], x_recv.at[me]
+    )
+    frame_copy = pltpu.make_async_copy(x_ref, x_frame, frame_sem)
+    wq0_local = pltpu.make_async_copy(wq_ref, wq0, w_sem.at[0])
+    wo0_local = pltpu.make_async_copy(wo_ref, wo0, w_sem.at[1])
+    wo1_local = pltpu.make_async_copy(wo_ref, wo1, w_sem.at[2])
+    wq1_local = [
+        pltpu.make_async_copy(wq_ref.at[:, wq1_cols(s, j)], wq1_dst(j), w_sem.at[3 + j])
+        for j in range(3)
+    ]
+    wq0_remote = pltpu.make_async_remote_copy(
+        wq_ref, wq0, w_send.at[0], w_sem.at[0], device_id=sibling, device_id_type=MESH
+    )
+    wo0_remote = pltpu.make_async_remote_copy(
+        wo_ref, wo0, w_send.at[1], w_sem.at[1], device_id=sibling, device_id_type=MESH
+    )
+    wq1_remote = [
+        pltpu.make_async_remote_copy(
+            wq_ref.at[:, wq1_cols(1 - s, j)],
+            wq1_dst(j),
+            w_send.at[2 + j],
+            w_sem.at[3 + j],
+            device_id=sibling,
+            device_id_type=MESH,
+        )
+        for j in range(3)
+    ]
+
+    pl.semaphore_wait(barrier, n)
+
+    def send_x(k, c):
+        x_copy(lax.rem(me + k, n), me).start()
+        return c
+
+    lax.fori_loop(1, n, send_x, 0)
+
+    @pl.when(s == 0)
+    def _():
+        wq0_remote.start()
+        wo0_remote.start()
+
+    own_x.start()
+
+    @pl.when(s == 0)
+    def _():
+        wq0_local.start()
+        wo0_local.start()
+
+    @pl.when(s == 1)
+    def _():
+        for copy in wq1_remote + wq1_local:
+            copy.start()
+        wo1_local.start()
+
+    frame_copy.start()
+
+    def norm_rows(k, c):
+        source = lax.rem(me + n - k, n)
+
+        @pl.when(k > 0)
+        def _():
+            x_copy(source, source).wait_recv()
+
+        @pl.when(k == 0)
+        def _():
+            own_x.wait()
+
+        x_norm[rows(source, half), :] = normalize(x_got[rows(source, half), :])
+        return c
+
+    lax.fori_loop(0, n, norm_rows, 0)
+
+    @pl.when(s == 0)
+    def _():
+        wq0_local.wait()
+
+    @pl.when(s == 1)
+    def _():
+        wq0_remote.wait_recv()
+
+    def project0(j, c):
+        columns = rows(j, 768)
+        qkv0[:, columns] = dot(x_norm[...], wq0[:, columns]).astype(jnp.bfloat16)
+        return c
+
+    lax.fori_loop(0, 3 * INNER // 768, project0, 0)
+
+    i0 = lax.broadcasted_iota(jnp.int32, (tokens, tokens), 0)
+    i1 = lax.broadcasted_iota(jnp.int32, (tokens, tokens), 1)
+    same = lax.rem(i0, half) == lax.rem(i1, half)
+    for h in range(HEADS):
+        q = qkv0[:, h * HDIM : (h + 1) * HDIM]
+        k = qkv0[:, INNER + h * HDIM : INNER + (h + 1) * HDIM]
+        v = qkv0[:, 2 * INNER + h * HDIM : 2 * INNER + (h + 1) * HDIM]
+        e = jnp.where(same, jnp.exp2(dot_t(q, k) * SCALE_LOG2), 0.0)
+        w = (e * (1.0 / jnp.sum(e, axis=-1, keepdims=True))).astype(jnp.bfloat16)
+        mix0[:, h * HDIM : (h + 1) * HDIM] = dot(w, v).astype(jnp.bfloat16)
+
+    def m_copy(f, source):
+        return pltpu.make_async_remote_copy(
+            src_ref=mix0.at[rows(f, half), :],
+            dst_ref=mix_frame.at[rows(2 * source + s, half), :],
+            send_sem=m_send.at[f],
+            recv_sem=m_recv.at[source],
+            device_id=peer(f),
+            device_id_type=MESH,
+        )
+
+    def f_copy(d, core):
+        return pltpu.make_async_remote_copy(
+            src_ref=mix_frame.at[rows(2 * d + core, half), :],
+            dst_ref=mix_frame.at[rows(2 * d + core, half), :],
+            send_sem=f_send.at[d],
+            recv_sem=f_recv.at[d],
+            device_id=sibling,
+            device_id_type=MESH,
+        )
+
+    def send_m(k, c):
+        m_copy(lax.rem(me + k, n), me).start()
+        return c
+
+    lax.fori_loop(1, n, send_m, 0)
+    mix_frame[rows(2 * me + s, half), :] = mix0[rows(me, half), :]
+    f_copy(me, s).start()
+
+    @pl.when(s == 0)
+    def _():
+        wo0_local.wait()
+
+    @pl.when(s == 1)
+    def _():
+        wo0_remote.wait_recv()
+
+    added = x_got[...].astype(jnp.float32) + dot(mix0[...], wo0[...])
+    first0[...] = added.astype(jnp.bfloat16).reshape(n, half, -1)
+    out_first = pltpu.make_async_copy(first0, out_ref.at[:, 0], out_sem.at[0])
+    out_remote = pltpu.make_async_remote_copy(
+        first0, out_ref.at[:, 1], out_send, out_recv, device_id=sibling, device_id_type=MESH
+    )
+
+    @pl.when(s == 0)
+    def _():
+        out_first.start()
+
+    @pl.when(s == 1)
+    def _():
+        out_remote.start()
+
+    frame_copy.wait()
+
+    def forward(k, c):
+        source = lax.rem(me + n - k, n)
+        m_copy(source, source).wait_recv()
+        f_copy(source, s).start()
+        return c
+
+    lax.fori_loop(1, n, forward, 0)
+
+    def forwarded(k, c):
+        f_copy(lax.rem(me + n - k, n), 1 - s).wait_recv()
+        return c
+
+    lax.fori_loop(0, n, forwarded, 0)
+    for j in range(3):
+
+        @pl.when(s == 0)
+        def _():
+            wq1_remote[j].wait_recv()
+
+        @pl.when(s == 1)
+        def _():
+            wq1_local[j].wait()
+
+    def middle(i, c):
+        part = rows(i, 256)
+        grown = x_frame[part, :].astype(jnp.float32) + dot(mix_frame[part, :], wo0[...])
+        grown = grown.astype(jnp.bfloat16)
+        first1[part, :] = grown
+        qkv1[part, :] = dot(normalize(grown), wq1[...]).astype(jnp.bfloat16)
+        return c
+
+    lax.fori_loop(0, tracks // 256, middle, 0)
+
+    r = lax.broadcasted_iota(jnp.int32, (BLOCK, tracks), 0)
+    t = lax.broadcasted_iota(jnp.int32, (BLOCK, tracks), 1)
+    track = lax.broadcasted_iota(jnp.int32, (1, tracks), 1)
+    block_of = track // BLOCK
+    seen = seen_ref[...] == 1
+
+    def low_copy(b):
+        return pltpu.make_async_remote_copy(
+            src_ref=mix1.at[rows(b, BLOCK), :],
+            dst_ref=mix1_low.at[rows(b, BLOCK), :],
+            send_sem=low_send.at[b],
+            recv_sem=low_recv.at[b],
+            device_id=sibling,
+            device_id_type=MESH,
+        )
+
+    def attend(b, c):
+        part = rows(b, BLOCK)
+        listed = (block_of == b) | (block_of == near_ref[b, 0]) | (block_of == near_ref[b, 1])
+        open_row = jnp.where(seen & listed, 1.0, 0.0)
+        allow = jnp.where(t == r + b * BLOCK, 1.0, open_row) > 0.5
+        for h in range(HALF_HEADS):
+            q = qkv1[part, h * HDIM : (h + 1) * HDIM]
+            k = qkv1[:, HALF_INNER + h * HDIM : HALF_INNER + (h + 1) * HDIM]
+            v = qkv1[:, 2 * HALF_INNER + h * HDIM : 2 * HALF_INNER + (h + 1) * HDIM]
+            e = jnp.where(allow, jnp.exp2(dot_t(q, k) * SCALE_LOG2), 0.0)
+            w = (e * (1.0 / jnp.sum(e, axis=-1, keepdims=True))).astype(jnp.bfloat16)
+            mix1[part, h * HDIM : (h + 1) * HDIM] = dot(w, v).astype(jnp.bfloat16)
+
+        @pl.when(s == 0)
+        def _():
+            low_copy(b).start()
+
+        return c
+
+    lax.fori_loop(0, blocks, attend, 0)
+    per_block = BLOCK // group
+
+    def out_copy(b):
+        return pltpu.make_async_copy(
+            second.at[rows(b, per_block)], out_ref.at[rows(b, per_block)], out_sem.at[1 + b]
+        )
+
+    @pl.when(s == 1)
+    def _():
+        wo1_local.wait()
+
+        def close(b, c):
+            part = rows(b, BLOCK)
+            low_copy(b).wait_recv()
+            delta = dot(mix1_low[part, :], wo1[:HALF_INNER, :]) + dot(
+                mix1[part, :], wo1[HALF_INNER:, :]
+            )
+            total = (first1[part, :].astype(jnp.float32) + delta).astype(jnp.bfloat16)
+            second[rows(b, per_block)] = total.reshape(per_block, 2, half, -1)
+            out_copy(b).start()
+            return c
+
+        lax.fori_loop(0, blocks, close, 0)
+
+        def closed(b, c):
+            out_copy(b).wait()
+            return c
+
+        lax.fori_loop(0, blocks, closed, 0)
+        out_remote.wait_send()
+        for copy in wq1_remote:
+            copy.wait_send()
+
+    @pl.when(s == 0)
+    def _():
+        out_first.wait()
+        out_remote.wait_recv()
+        wq0_remote.wait_send()
+        wo0_remote.wait_send()
+
+        def sent_low(b, c):
+            low_copy(b).wait_send()
+            return c
+
+        lax.fori_loop(0, blocks, sent_low, 0)
+
+    def drain(k, c):
+        d = lax.rem(me + k, n)
+        x_copy(d, me).wait_send()
+        m_copy(d, me).wait_send()
+        f_copy(d, s).wait_send()
+        return c
+
+    lax.fori_loop(1, n, drain, 0)
+    f_copy(me, s).wait_send()
+
+
+def on_device_fused(tracks_in, w_qkv, w_out, visible, neighbours):
+    n = lax.axis_size("seq")
+    tracks, width = tracks_in.shape[2:]
+    half = tracks // n // 2
+    tokens = n * half
+    blocks = tracks // BLOCK
+    bf16 = jnp.bfloat16
+    dma = pltpu.SemaphoreType.DMA
+    anywhere = pl.BlockSpec(memory_space=pl.ANY)
+    out = pl.pallas_call(
+        functools.partial(fused_kernel, n, half),
+        out_shape=jax.ShapeDtypeStruct((n, 2, half, width), bf16),
+        in_specs=[anywhere] * 3
+        + [pl.BlockSpec(memory_space=pltpu.VMEM), pl.BlockSpec(memory_space=pltpu.SMEM)],
+        out_specs=anywhere,
+        scratch_shapes=[
+            pltpu.VMEM((width, 3 * INNER), bf16),
+            pltpu.VMEM((INNER, width), bf16),
+            pltpu.VMEM((width, 3 * HALF_INNER), bf16),
+            pltpu.VMEM((INNER, width), bf16),
+            pltpu.VMEM((tokens, width), bf16),
+            pltpu.VMEM((tokens, width), bf16),
+            pltpu.VMEM((tracks, width), bf16),
+            pltpu.VMEM((tokens, 3 * INNER), bf16),
+            pltpu.VMEM((tokens, INNER), bf16),
+            pltpu.VMEM((n, half, width), bf16),
+            pltpu.VMEM((tracks, INNER), bf16),
+            pltpu.VMEM((tracks, width), bf16),
+            pltpu.VMEM((tracks, 3 * HALF_INNER), bf16),
+            pltpu.VMEM((tracks, HALF_INNER), bf16),
+            pltpu.VMEM((tracks, HALF_INNER), bf16),
+            pltpu.VMEM((n, 2, half, width), bf16),
+            dma((6,)),
+            dma((5,)),
+            dma((n,)),
+            dma((n,)),
+            dma,
+            dma((n,)),
+            dma((n,)),
+            dma((n,)),
+            dma((n,)),
+            dma((blocks,)),
+            dma((blocks,)),
+            dma((1 + blocks,)),
+            dma,
+            dma,
+        ],
+        compiler_params=pltpu.CompilerParams(
+            collective_id=0, has_side_effects=True, vmem_limit_bytes=56 * 1024 * 1024
+        ),
+        cost_estimate=pl.CostEstimate(
+            flops=9_000_000_000, bytes_accessed=20_000_000, transcendentals=1_200_000
+        ),
+    )(
+        tracks_in.reshape(tracks, width),
+        w_qkv.reshape(width, 3 * INNER),
+        w_out.reshape(INNER, width),
+        visible.reshape(1, tracks),
+        neighbours.reshape(blocks, NB),
+    )
+    return out.reshape(1, 1, 1, tracks, width)
+
+
+def fits_fused(mesh):
+    return mesh.shape["seq"] == FRAMES and mesh.shape["segment"] == 2
+
+
 def solution(mesh):
+    body = on_device_fused if fits_fused(mesh) else on_device
     return jax.shard_map(
-        on_device,
+        body,
         mesh=mesh,
         in_specs=(
             P(None, "seq", None, None),

time: 155 us -> 54.4 us (0.35)
  Pallas kernels: 0 us -> 49.8 us
  waiting for transfers between devices: 49.2 us -> 0 us
  blocking collectives: 26 us -> 0 us
  local copies, waits for them, and re-layouts: 28 us -> 3.99 us
  matrix products: 19.8 us -> 0 us
  between operations: 13.6 us -> 0.01 us
  other arithmetic: 8.69 us -> 0 us
  starting transfers between devices: 8.15 us -> 0 us
    pallas_call x0 -> x1, Pallas kernels: none -> 49.8 us  [on_device_fused(): pl.pallas_call(functools.partial(fused_kernel, n, half), out_shape=jax.Sh...]
    all_to_all x1 -> x0, waiting for transfers between devices: 33.5 us -> none  [on_device(): lax.all_to_all(full_first, 'seq', split_axis=0, concat_axis=0, tiled=True)]
    all_to_all x1 -> x0, blocking collectives: 26 us -> none  [on_device(): moved = lax.all_to_all(mine, 'seq', split_axis=0, concat_axis=0, tiled=True)]
    dot_general x7 -> x0, matrix products: 19.3 us -> none  [the longest x2 14 us: project(): jnp.dot(normalize(tokens), weight, preferred_element_type=jnp.float32)]
    all_gather x2 -> x0, waiting for transfers between devices: 8.18 us -> none  [the longest x1 5.47 us: on_device(): lax.all_gather(w_out, 'segment', axis=0, tiled=True)]
    reshape x2 -> x1, local copies, waits for them, and re-layouts: 8.14 us -> 1.34 us  [on_device_fused(): neighbours.reshape(blocks, NB)]
    all_to_all x1 -> x0, starting transfers between devices: 6.54 us -> none  [on_device(): lax.all_to_all(full_first, 'seq', split_axis=0, concat_axis=0, tiled=True)]
    ppermute x2 -> x0, waiting for transfers between devices: 6.08 us -> none  [the longest x1 4.01 us: from_behind(): lax.ppermute(value, axis, [(source, source + steps) for source in range(i...]
  transfers between devices with their start and end apart: 5 -> 0, of which waited for: 5 -> 0; matrix products, arithmetic and copies ran while one was open for 9% -> 0% of each run, Pallas kernels for 0% -> 0%
where the time goes in v1:
time: 54.4 us; the launch traced here: 53.8 us
  Pallas kernels  49.8 us (92%)
  local copies, waits for them, and re-layouts  3.99 us (7%)
    pallas_call x1, Pallas kernels, on_device_fused(): pl.pallas_call(functools.partial(fused_kernel, n, half), out_shape=jax.Sh...  49.8 us
    unnamed x1, local copies, waits for them, and re-layouts  2.65 us
    reshape x1, local copies, waits for them, and re-layouts, on_device_fused(): neighbours.reshape(blocks, NB)  1.34 us

profile of v1, /device:TPU:9, one launch (start us, length us, event | category | flops | bytes accessed | tf_op | source)
XLA Modules:
  0.0 53.8 jit_solution(12549994112248192929)
XLA Ops:
  0.0 1.3 %copy.6.near_ref = s32[4,2]{1,0:T(4,128)} copy(s32[4,2]{0,1:T(2,128)} %bitcast.7) | data formatting | bytes 64 | tf_op jit(solution)/shard_map/reshape | solution.py:570
  1.3 49.8 %shard_map.55 = bf16[16,2,16,1536]{3,2,1,0:T(8,128)(2,1)} custom-call(bf16[512,1536]{1,0:T(8,128)(2,1)} %bitcast.10, bf16[1536,2304]{1,0:T(8,128)(2,1)} %bitcast.8, bf16[768,1536]{1,0:T(8,128)(2,1)} %bitcast.9, s32[1,512]{1,0:T(1,128)} %bitcast.11, s32[4,2]{1,0:T(4,128)} %copy.6.near_ref), custom_call_target="tpu_custom_call" | custom-call | flops 8999999488 | bytes 20000000 | tf_op jit(solution)/shard_map/pallas_call | solution.py:521
  51.1 2.7 %copy.8 = bf16[1,1,1,512,1536]{4,3,2,1,0:T(8,128)(2,1)} copy(bf16[1,1,1,512,1536]{4,3,2,1,0:T(8,128)(2,1)} %bitcast.6) | data formatting | bytes 3145728

commit v2 on v1

--- a/solution.py
+++ b/solution.py
@@ -175,20 +175,26 @@
     mix1,
     mix1_low,
     second,
-    w_sem,
-    w_send,
+    wq0_sem,
+    wq0_send,
+    wq1_sem,
+    wq1_send,
+    wo_sem,
+    wo_send,
     x_send,
     x_recv,
+    xf_send,
+    xf_recv,
     frame_sem,
     m_send,
     m_recv,
     f_send,
     f_recv,
+    up_send,
+    up_recv,
     low_send,
     low_recv,
     out_sem,
-    out_send,
-    out_recv,
 ):
     s = lax.axis_index("segment")
     me = lax.axis_index("seq")
@@ -215,50 +221,73 @@
     def rows(index, size):
         return pl.ds(pl.multiple_of(index * size, size), size)
 
+    def local(src, dst, sem):
+        return pltpu.make_async_copy(src, dst, sem)
+
+    def remote(src, dst, send, recv, device):
+        return pltpu.make_async_remote_copy(
+            src_ref=src,
+            dst_ref=dst,
+            send_sem=send,
+            recv_sem=recv,
+            device_id=device,
+            device_id_type=MESH,
+        )
+
     def x_copy(d, source):
-        return pltpu.make_async_remote_copy(
-            src_ref=x_ref.at[rows(2 * d + s, half), :],
-            dst_ref=x_got.at[rows(source, half), :],
-            send_sem=x_send.at[d],
-            recv_sem=x_recv.at[source],
-            device_id=peer(d),
-            device_id_type=MESH,
-        )
-
-    def wq1_cols(core, j):
+        return remote(
+            x_ref.at[rows(2 * d + s, half), :],
+            x_got.at[rows(s * n + source, half), :],
+            x_send.at[d],
+            x_recv.at[source],
+            peer(d),
+        )
+
+    def xf_copy(source, core):
+        place = rows(core * n + source, half)
+        return remote(
+            x_got.at[place, :], x_got.at[place, :], xf_send.at[source], xf_recv.at[source], sibling
+        )
+
+    def head_cols(core, j):
         return pl.ds(pl.multiple_of(j * INNER + core * HALF_INNER, HDIM), HALF_INNER)
 
-    def wq1_dst(j):
-        return wq1.at[:, pl.ds(j * HALF_INNER, HALF_INNER)]
-
-    own_x = pltpu.make_async_copy(
-        x_ref.at[rows(2 * me + s, half), :], x_got.at[rows(me, half), :], x_recv.at[me]
-    )
-    frame_copy = pltpu.make_async_copy(x_ref, x_frame, frame_sem)
-    wq0_local = pltpu.make_async_copy(wq_ref, wq0, w_sem.at[0])
-    wo0_local = pltpu.make_async_copy(wo_ref, wo0, w_sem.at[1])
-    wo1_local = pltpu.make_async_copy(wo_ref, wo1, w_sem.at[2])
+    def packed(w, j):
+        return w.at[:, pl.ds(j * HALF_INNER, HALF_INNER)]
+
+    own_x = local(
+        x_ref.at[rows(2 * me + s, half), :], x_got.at[rows(s * n + me, half), :], x_recv.at[me]
+    )
+    frame_copy = local(x_ref, x_frame, frame_sem)
+    wq0_local = [
+        local(wq_ref.at[:, head_cols(s, j)], packed(wq0, j), wq0_sem.at[j]) for j in range(3)
+    ]
     wq1_local = [
-        pltpu.make_async_copy(wq_ref.at[:, wq1_cols(s, j)], wq1_dst(j), w_sem.at[3 + j])
+        local(wq_ref.at[:, head_cols(s, j)], packed(wq1, j), wq1_sem.at[j]) for j in range(3)
+    ]
+    wq0_remote = [
+        remote(
+            wq_ref.at[:, head_cols(1 - s, j)],
+            packed(wq0, j),
+            wq0_send.at[j],
+            wq0_sem.at[j],
+            sibling,
+        )
         for j in range(3)
     ]
-    wq0_remote = pltpu.make_async_remote_copy(
-        wq_ref, wq0, w_send.at[0], w_sem.at[0], device_id=sibling, device_id_type=MESH
-    )
-    wo0_remote = pltpu.make_async_remote_copy(
-        wo_ref, wo0, w_send.at[1], w_sem.at[1], device_id=sibling, device_id_type=MESH
-    )
     wq1_remote = [
-        pltpu.make_async_remote_copy(
-            wq_ref.at[:, wq1_cols(1 - s, j)],
-            wq1_dst(j),
-            w_send.at[2 + j],
-            w_sem.at[3 + j],
-            device_id=sibling,
-            device_id_type=MESH,
+        remote(
+            wq_ref.at[:, head_cols(1 - s, j)],
+            packed(wq1, j),
+            wq1_send.at[j],
+            wq1_sem.at[j],
+            sibling,
         )
         for j in range(3)
     ]
+    wo0_local = local(wo_ref, wo0, wo_sem.at[0])
+    wo1_local = local(wo_ref, wo1, wo_sem.at[1])
+    wo0_remote = remote(wo_ref, wo0, wo_send, wo_sem.at[0], sibling)
 
     pl.semaphore_wait(barrier, n)
 
@@ -267,17 +296,13 @@
         return c
 
     lax.fori_loop(1, n, send_x, 0)
+    own_x.start()
 
     @pl.when(s == 0)
     def _():
-        wq0_remote.start()
+        for copy in wq0_remote + wq0_local:
+            copy.start()
         wo0_remote.start()
-
-    own_x.start()
-
-    @pl.when(s == 0)
-    def _():
-        wq0_local.start()
         wo0_local.start()
 
     @pl.when(s == 1)
@@ -288,7 +313,7 @@
 
     frame_copy.start()
 
-    def norm_rows(k, c):
+    def take_x(k, c):
         source = lax.rem(me + n - k, n)
 
         @pl.when(k > 0)
@@ -299,64 +324,87 @@
         def _():
             own_x.wait()
 
-        x_norm[rows(source, half), :] = normalize(x_got[rows(source, half), :])
-        return c
-
-    lax.fori_loop(0, n, norm_rows, 0)
-
-    @pl.when(s == 0)
-    def _():
-        wq0_local.wait()
-
-    @pl.when(s == 1)
-    def _():
-        wq0_remote.wait_recv()
-
-    def project0(j, c):
-        columns = rows(j, 768)
-        qkv0[:, columns] = dot(x_norm[...], wq0[:, columns]).astype(jnp.bfloat16)
-        return c
-
-    lax.fori_loop(0, 3 * INNER // 768, project0, 0)
+        xf_copy(source, s).start()
+        place = rows(s * n + source, half)
+        x_norm[place, :] = normalize(x_got[place, :])
+        return c
+
+    def take_xf(k, c):
+        source = lax.rem(me + n - k, n)
+        xf_copy(source, 1 - s).wait_recv()
+        place = rows((1 - s) * n + source, half)
+        x_norm[place, :] = normalize(x_got[place, :])
+        return c
+
+    lax.fori_loop(0, n, take_x, 0)
+    for j in range(3):
+
+        @pl.when(s == 0)
+        def _():
+            wq0_local[j].wait()
+
+        @pl.when(s == 1)
+        def _():
+            wq0_remote[j].wait_recv()
 
     i0 = lax.broadcasted_iota(jnp.int32, (tokens, tokens), 0)
     i1 = lax.broadcasted_iota(jnp.int32, (tokens, tokens), 1)
     same = lax.rem(i0, half) == lax.rem(i1, half)
-    for h in range(HEADS):
-        q = qkv0[:, h * HDIM : (h + 1) * HDIM]
-        k = qkv0[:, INNER + h * HDIM : INNER + (h + 1) * HDIM]
-        v = qkv0[:, 2 * INNER + h * HDIM : 2 * INNER + (h + 1) * HDIM]
-        e = jnp.where(same, jnp.exp2(dot_t(q, k) * SCALE_LOG2), 0.0)
-        w = (e * (1.0 / jnp.sum(e, axis=-1, keepdims=True))).astype(jnp.bfloat16)
-        mix0[:, h * HDIM : (h + 1) * HDIM] = dot(w, v).astype(jnp.bfloat16)
-
-    def m_copy(f, source):
-        return pltpu.make_async_remote_copy(
-            src_ref=mix0.at[rows(f, half), :],
-            dst_ref=mix_frame.at[rows(2 * source + s, half), :],
-            send_sem=m_send.at[f],
-            recv_sem=m_recv.at[source],
-            device_id=peer(f),
-            device_id_type=MESH,
-        )
-
-    def f_copy(d, core):
-        return pltpu.make_async_remote_copy(
-            src_ref=mix_frame.at[rows(2 * d + core, half), :],
-            dst_ref=mix_frame.at[rows(2 * d + core, half), :],
-            send_sem=f_send.at[d],
-            recv_sem=f_recv.at[d],
-            device_id=sibling,
-            device_id_type=MESH,
-        )
-
-    def send_m(k, c):
-        m_copy(lax.rem(me + k, n), me).start()
-        return c
-
-    lax.fori_loop(1, n, send_m, 0)
-    mix_frame[rows(2 * me + s, half), :] = mix0[rows(me, half), :]
-    f_copy(me, s).start()
+    own_cols = pl.ds(pl.multiple_of(s * HALF_INNER, HDIM), HALF_INNER)
+
+    def m_copy(f, source, g):
+        return remote(
+            mix0.at[rows(g * n + f, half), own_cols],
+            mix_frame.at[rows(2 * source + g, half), own_cols],
+            m_send.at[g * n + f],
+            m_recv.at[g * n + source],
+            peer(f),
+        )
+
+    def f_copy(d, core, g):
+        place = mix_frame.at[
+            rows(2 * d + g, half), pl.ds(pl.multiple_of(core * HALF_INNER, HDIM), HALF_INNER)
+        ]
+        return remote(place, place, f_send.at[g * n + d], f_recv.at[g * n + d], sibling)
+
+    def up_copy(g):
+        place = mix0.at[rows(g, tokens), pl.ds(HALF_INNER, HALF_INNER)]
+        return remote(place, place, up_send.at[g], up_recv.at[g], sibling)
+
+    def time_half(order, c):
+        g = jnp.where(order == 0, s, 1 - s)
+        part = rows(g, tokens)
+
+        @pl.when(order == 1)
+        def _():
+            lax.fori_loop(0, n, take_xf, 0)
+
+        qkv0[...] = dot(x_norm[part, :], wq0[...]).astype(jnp.bfloat16)
+        mixed = []
+        for h in range(HALF_HEADS):
+            q = qkv0[:, h * HDIM : (h + 1) * HDIM]
+            k = qkv0[:, HALF_INNER + h * HDIM : HALF_INNER + (h + 1) * HDIM]
+            v = qkv0[:, 2 * HALF_INNER + h * HDIM : 2 * HALF_INNER + (h + 1) * HDIM]
+            e = jnp.where(same, jnp.exp2(dot_t(q, k) * SCALE_LOG2), 0.0)
+            w = (e * (1.0 / jnp.sum(e, axis=-1, keepdims=True))).astype(jnp.bfloat16)
+            mixed.append(dot(w, v).astype(jnp.bfloat16))
+        mix0[part, own_cols] = jnp.concatenate(mixed, axis=1)
+
+        def send_m(k, c):
+            m_copy(lax.rem(me + k, n), me, g).start()
+            return c
+
+        lax.fori_loop(1, n, send_m, 0)
+        mix_frame[rows(2 * me + g, half), own_cols] = mix0[rows(g * n + me, half), own_cols]
+        f_copy(me, s, g).start()
+
+        @pl.when(s == 1)
+        def _():
+            up_copy(g).start()
+
+        return c
+
+    lax.fori_loop(0, 2, time_half, 0)
 
     @pl.when(s == 0)
     def _():
@@ -366,36 +414,40 @@
     def _():
         wo0_remote.wait_recv()
 
-    added = x_got[...].astype(jnp.float32) + dot(mix0[...], wo0[...])
-    first0[...] = added.astype(jnp.bfloat16).reshape(n, half, -1)
-    out_first = pltpu.make_async_copy(first0, out_ref.at[:, 0], out_sem.at[0])
-    out_remote = pltpu.make_async_remote_copy(
-        first0, out_ref.at[:, 1], out_send, out_recv, device_id=sibling, device_id_type=MESH
-    )
+    def forward(i, c):
+        g = jnp.where(i < n - 1, s, 1 - s)
+        source = lax.rem(me + n - 1 - lax.rem(i, n - 1), n)
+        m_copy(source, source, g).wait_recv()
+        f_copy(source, s, g).start()
+        return c
+
+    lax.fori_loop(0, n - 1, forward, 0)
+
+    def first_out(g):
+        return local(first0.at[g], out_ref.at[:, g], out_sem.at[blocks + g])
 
     @pl.when(s == 0)
     def _():
-        out_first.start()
-
-    @pl.when(s == 1)
-    def _():
-        out_remote.start()
-
+        def give(i, c):
+            g = 1 - i
+            up_copy(g).wait_recv()
+            part = rows(g, tokens)
+            added = x_got[part, :].astype(jnp.float32) + dot(mix0[part, :], wo0[...])
+            first0[g] = added.astype(jnp.bfloat16).reshape(n, half, -1)
+            first_out(g).start()
+            return c
+
+        lax.fori_loop(0, 2, give, 0)
+
+    lax.fori_loop(n - 1, 2 * (n - 1), forward, 0)
     frame_copy.wait()
 
-    def forward(k, c):
-        source = lax.rem(me + n - k, n)
-        m_copy(source, source).wait_recv()
-        f_copy(source, s).start()
-        return c
-
-    lax.fori_loop(1, n, forward, 0)
-
-    def forwarded(k, c):
-        f_copy(lax.rem(me + n - k, n), 1 - s).wait_recv()
-        return c
-
-    lax.fori_loop(0, n, forwarded, 0)
+    def forwarded(i, c):
+        g = jnp.where(i < n, 1 - s, s)
+        f_copy(lax.rem(me + n - lax.rem(i, n), n), 1 - s, g).wait_recv()
+        return c
+
+    lax.fori_loop(0, 2 * n, forwarded, 0)
     for j in range(3):
 
         @pl.when(s == 0)
@@ -418,23 +470,20 @@
 
     r = lax.broadcasted_iota(jnp.int32, (BLOCK, tracks), 0)
     t = lax.broadcasted_iota(jnp.int32, (BLOCK, tracks), 1)
-    track = lax.broadcasted_iota(jnp.int32, (1, tracks), 1)
-    block_of = track // BLOCK
+    block_of = lax.broadcasted_iota(jnp.int32, (1, tracks), 1) // BLOCK
+    near_at = lax.broadcasted_iota(jnp.int32, (NB, blocks), 1)
     seen = seen_ref[...] == 1
 
     def low_copy(b):
-        return pltpu.make_async_remote_copy(
-            src_ref=mix1.at[rows(b, BLOCK), :],
-            dst_ref=mix1_low.at[rows(b, BLOCK), :],
-            send_sem=low_send.at[b],
-            recv_sem=low_recv.at[b],
-            device_id=sibling,
-            device_id_type=MESH,
+        place = rows(b, BLOCK)
+        return remote(
+            mix1.at[place, :], mix1_low.at[place, :], low_send.at[b], low_recv.at[b], sibling
         )
 
     def attend(b, c):
         part = rows(b, BLOCK)
-        listed = (block_of == b) | (block_of == near_ref[b, 0]) | (block_of == near_ref[b, 1])
+        near = jnp.sum(jnp.where(near_at == b, near_ref[...], 0), axis=1, keepdims=True)
+        listed = (block_of == b) | (block_of == near[0:1]) | (block_of == near[1:2])
         open_row = jnp.where(seen & listed, 1.0, 0.0)
         allow = jnp.where(t == r + b * BLOCK, 1.0, open_row) > 0.5
         for h in range(HALF_HEADS):
@@ -455,9 +504,7 @@
     per_block = BLOCK // group
 
     def out_copy(b):
-        return pltpu.make_async_copy(
-            second.at[rows(b, per_block)], out_ref.at[rows(b, per_block)], out_sem.at[1 + b]
-        )
+        return local(second.at[rows(b, per_block)], out_ref.at[rows(b, per_block)], out_sem.at[b])
 
     @pl.when(s == 1)
     def _():
@@ -466,11 +513,11 @@
         def close(b, c):
             part = rows(b, BLOCK)
             low_copy(b).wait_recv()
-            delta = dot(mix1_low[part, :], wo1[:HALF_INNER, :]) + dot(
-                mix1[part, :], wo1[HALF_INNER:, :]
+            mixed = jnp.concatenate([mix1_low[part, :], mix1[part, :]], axis=1)
+            total = first1[part, :].astype(jnp.float32) + dot(mixed, wo1[...])
+            second[rows(b, per_block)] = total.astype(jnp.bfloat16).reshape(
+                per_block, 2, half, -1
             )
-            total = (first1[part, :].astype(jnp.float32) + delta).astype(jnp.bfloat16)
-            second[rows(b, per_block)] = total.reshape(per_block, 2, half, -1)
             out_copy(b).start()
             return c
 
@@ -481,16 +528,17 @@
             return c
 
         lax.fori_loop(0, blocks, closed, 0)
-        out_remote.wait_send()
         for copy in wq1_remote:
             copy.wait_send()
+        for g in range(2):
+            up_copy(g).wait_send()
 
     @pl.when(s == 0)
     def _():
-        out_first.wait()
-        out_remote.wait_recv()
-        wq0_remote.wait_send()
-        wo0_remote.wait_send()
+        for g in range(2):
+            first_out(g).wait()
+        for copy in wq0_remote + [wo0_remote]:
+            copy.wait_send()
 
         def sent_low(b, c):
             low_copy(b).wait_send()
@@ -500,13 +548,19 @@
 
     def drain(k, c):
         d = lax.rem(me + k, n)
-        x_copy(d, me).wait_send()
-        m_copy(d, me).wait_send()
-        f_copy(d, s).wait_send()
-        return c
-
-    lax.fori_loop(1, n, drain, 0)
-    f_copy(me, s).wait_send()
+
+        @pl.when(k > 0)
+        def _():
+            x_copy(d, me).wait_send()
+            m_copy(d, me, 0).wait_send()
+            m_copy(d, me, 1).wait_send()
+
+        xf_copy(d, s).wait_send()
+        f_copy(d, s, 0).wait_send()
+        f_copy(d, s, 1).wait_send()
+        return c
+
+    lax.fori_loop(0, n, drain, 0)
 
 
 def on_device_fused(tracks_in, w_qkv, w_out, visible, neighbours):
@@ -518,43 +572,49 @@
     bf16 = jnp.bfloat16
     dma = pltpu.SemaphoreType.DMA
     anywhere = pl.BlockSpec(memory_space=pl.ANY)
+    in_vmem = pl.BlockSpec(memory_space=pltpu.VMEM)
     out = pl.pallas_call(
         functools.partial(fused_kernel, n, half),
         out_shape=jax.ShapeDtypeStruct((n, 2, half, width), bf16),
-        in_specs=[anywhere] * 3
-        + [pl.BlockSpec(memory_space=pltpu.VMEM), pl.BlockSpec(memory_space=pltpu.SMEM)],
+        in_specs=[anywhere] * 3 + [in_vmem] * 2,
         out_specs=anywhere,
         scratch_shapes=[
-            pltpu.VMEM((width, 3 * INNER), bf16),
+            pltpu.VMEM((width, 3 * HALF_INNER), bf16),
             pltpu.VMEM((INNER, width), bf16),
             pltpu.VMEM((width, 3 * HALF_INNER), bf16),
             pltpu.VMEM((INNER, width), bf16),
-            pltpu.VMEM((tokens, width), bf16),
-            pltpu.VMEM((tokens, width), bf16),
             pltpu.VMEM((tracks, width), bf16),
-            pltpu.VMEM((tokens, 3 * INNER), bf16),
-            pltpu.VMEM((tokens, INNER), bf16),
-            pltpu.VMEM((n, half, width), bf16),
+            pltpu.VMEM((tracks, width), bf16),
+            pltpu.VMEM((tracks, width), bf16),
+            pltpu.VMEM((tokens, 3 * HALF_INNER), bf16),
+            pltpu.VMEM((tracks, INNER), bf16),
+            pltpu.VMEM((2, n, half, width), bf16),
             pltpu.VMEM((tracks, INNER), bf16),
             pltpu.VMEM((tracks, width), bf16),
             pltpu.VMEM((tracks, 3 * HALF_INNER), bf16),
             pltpu.VMEM((tracks, HALF_INNER), bf16),
             pltpu.VMEM((tracks, HALF_INNER), bf16),
             pltpu.VMEM((n, 2, half, width), bf16),
-            dma((6,)),
-            dma((5,)),
-            dma((n,)),
-            dma((n,)),
+            dma((3,)),
+            dma((3,)),
+            dma((3,)),
+            dma((3,)),
+            dma((2,)),
             dma,
             dma((n,)),
             dma((n,)),
             dma((n,)),
             dma((n,)),
+            dma,
+            dma((2 * n,)),
+            dma((2 * n,)),
+            dma((2 * n,)),
+            dma((2 * n,)),
+            dma((2,)),
+            dma((2,)),
             dma((blocks,)),
             dma((blocks,)),
-            dma((1 + blocks,)),
-            dma,
-            dma,
+            dma((blocks + 2,)),
         ],
         compiler_params=pltpu.CompilerParams(
             collective_id=0, has_side_effects=True, vmem_limit_bytes=56 * 1024 * 1024
@@ -567,7 +627,7 @@
         w_qkv.reshape(width, 3 * INNER),
         w_out.reshape(INNER, width),
         visible.reshape(1, tracks),
-        neighbours.reshape(blocks, NB),
+        neighbours.reshape(blocks, NB).T,
     )
     return out.reshape(1, 1, 1, tracks, width)
 

time: 54.4 us -> 59.5 us (1.094)
  the two profiles are of different devices: /device:TPU:9 before, /device:TPU:1 now
where the time goes in v2:
time: 59.5 us; the launch traced here: 59.3 us
  Pallas kernels  56.6 us (95%)
  local copies, waits for them, and re-layouts  2.65 us (4%)
    pallas_call x1, Pallas kernels, on_device_fused(): pl.pallas_call(functools.partial(fused_kernel, n, half), out_shape=jax.Sh...  56.6 us
    unnamed x1, local copies, waits for them, and re-layouts  2.65 us

profile of v2, /device:TPU:1, one launch (start us, length us, event | category | flops | bytes accessed | tf_op | source)
XLA Modules:
  0.0 59.3 jit_solution(773132880542426752)
XLA Ops:
  0.0 56.6 %shard_map.55 = bf16[16,2,16,1536]{3,2,1,0:T(8,128)(2,1)} custom-call(bf16[512,1536]{1,0:T(8,128)(2,1)} %bitcast.11, bf16[1536,2304]{1,0:T(8,128)(2,1)} %bitcast.9, bf16[768,1536]{1,0:T(8,128)(2,1)} %bitcast.10, s32[1,512]{1,0:T(1,128)} %bitcast.12, s32[2,4]{1,0:T(2,128)} %bitcast.13), custom_call_target="tpu_custom_call" | custom-call | flops 8999999488 | bytes 20000000 | tf_op jit(solution)/shard_map/pallas_call | solution.py:576
  56.6 2.7 %copy.7 = bf16[1,1,1,512,1536]{4,3,2,1,0:T(8,128)(2,1)} copy(bf16[1,1,1,512,1536]{4,3,2,1,0:T(8,128)(2,1)} %bitcast.8) | data formatting | bytes 3145728

commit v3 on v1

--- a/solution.py
+++ b/solution.py
@@ -174,7 +174,6 @@
     qkv1,
     mix1,
     mix1_low,
-    second,
     w_sem,
     w_send,
     x_send,
@@ -186,7 +185,6 @@
     f_recv,
     low_send,
     low_recv,
-    out_sem,
     out_send,
     out_recv,
 ):
@@ -200,6 +198,14 @@
 
     def peer(d):
         return {"segment": s, "seq": d}
+
+    def partner_at(k):
+        bit, d = 1, 0
+        while bit < n:
+            mine = lax.rem(me // bit, 2)
+            d = d + bit * lax.rem(mine + lax.rem(k // bit, 2), 2)
+            bit *= 2
+        return d
 
     barrier = pltpu.get_barrier_semaphore()
 
@@ -263,7 +269,7 @@
     pl.semaphore_wait(barrier, n)
 
     def send_x(k, c):
-        x_copy(lax.rem(me + k, n), me).start()
+        x_copy(partner_at(n - k), me).start()
         return c
 
     lax.fori_loop(1, n, send_x, 0)
@@ -289,7 +295,7 @@
     frame_copy.start()
 
     def norm_rows(k, c):
-        source = lax.rem(me + n - k, n)
+        source = partner_at(k)
 
         @pl.when(k > 0)
         def _():
@@ -302,22 +308,22 @@
         x_norm[rows(source, half), :] = normalize(x_got[rows(source, half), :])
         return c
 
-    lax.fori_loop(0, n, norm_rows, 0)
-
-    @pl.when(s == 0)
-    def _():
-        wq0_local.wait()
-
-    @pl.when(s == 1)
-    def _():
-        wq0_remote.wait_recv()
-
-    def project0(j, c):
-        columns = rows(j, 768)
-        qkv0[:, columns] = dot(x_norm[...], wq0[:, columns]).astype(jnp.bfloat16)
-        return c
-
-    lax.fori_loop(0, 3 * INNER // 768, project0, 0)
+    def project0(i, c):
+        lax.fori_loop(i * (n // 2), (i + 1) * (n // 2), norm_rows, 0)
+
+        @pl.when((i == 0) & (s == 0))
+        def _():
+            wq0_local.wait()
+
+        @pl.when((i == 0) & (s == 1))
+        def _():
+            wq0_remote.wait_recv()
+
+        part = rows(lax.rem(me // (n // 2) + i, 2), tokens // 2)
+        qkv0[part, :] = dot(x_norm[part, :], wq0[...]).astype(jnp.bfloat16)
+        return c
+
+    lax.fori_loop(0, 2, project0, 0)
 
     i0 = lax.broadcasted_iota(jnp.int32, (tokens, tokens), 0)
     i1 = lax.broadcasted_iota(jnp.int32, (tokens, tokens), 1)
@@ -333,30 +339,33 @@
     def m_copy(f, source):
         return pltpu.make_async_remote_copy(
             src_ref=mix0.at[rows(f, half), :],
-            dst_ref=mix_frame.at[rows(2 * source + s, half), :],
+            dst_ref=mix_frame.at[rows(s * n + source, half), :],
             send_sem=m_send.at[f],
             recv_sem=m_recv.at[source],
             device_id=peer(f),
             device_id_type=MESH,
         )
 
-    def f_copy(d, core):
+    per_block = BLOCK // group
+    gathered = per_block * half
+
+    def f_copy(b, core):
+        place = rows(core * blocks + b, gathered)
         return pltpu.make_async_remote_copy(
-            src_ref=mix_frame.at[rows(2 * d + core, half), :],
-            dst_ref=mix_frame.at[rows(2 * d + core, half), :],
-            send_sem=f_send.at[d],
-            recv_sem=f_recv.at[d],
+            src_ref=mix_frame.at[place, :],
+            dst_ref=mix_frame.at[place, :],
+            send_sem=f_send.at[b],
+            recv_sem=f_recv.at[b],
             device_id=sibling,
             device_id_type=MESH,
         )
 
     def send_m(k, c):
-        m_copy(lax.rem(me + k, n), me).start()
+        m_copy(partner_at(n - k), me).start()
         return c
 
     lax.fori_loop(1, n, send_m, 0)
-    mix_frame[rows(2 * me + s, half), :] = mix0[rows(me, half), :]
-    f_copy(me, s).start()
+    mix_frame[rows(s * n + me, half), :] = mix0[rows(me, half), :]
 
     @pl.when(s == 0)
     def _():
@@ -367,35 +376,21 @@
         wo0_remote.wait_recv()
 
     added = x_got[...].astype(jnp.float32) + dot(mix0[...], wo0[...])
-    first0[...] = added.astype(jnp.bfloat16).reshape(n, half, -1)
-    out_first = pltpu.make_async_copy(first0, out_ref.at[:, 0], out_sem.at[0])
+    added = added.astype(jnp.bfloat16).reshape(n, half, -1)
     out_remote = pltpu.make_async_remote_copy(
         first0, out_ref.at[:, 1], out_send, out_recv, device_id=sibling, device_id_type=MESH
     )
 
     @pl.when(s == 0)
     def _():
-        out_first.start()
+        out_ref[:, 0] = added
 
     @pl.when(s == 1)
     def _():
+        first0[...] = added
         out_remote.start()
 
     frame_copy.wait()
-
-    def forward(k, c):
-        source = lax.rem(me + n - k, n)
-        m_copy(source, source).wait_recv()
-        f_copy(source, s).start()
-        return c
-
-    lax.fori_loop(1, n, forward, 0)
-
-    def forwarded(k, c):
-        f_copy(lax.rem(me + n - k, n), 1 - s).wait_recv()
-        return c
-
-    lax.fori_loop(0, n, forwarded, 0)
     for j in range(3):
 
         @pl.when(s == 0)
@@ -407,19 +402,34 @@
             wq1_local[j].wait()
 
     def middle(i, c):
-        part = rows(i, 256)
-        grown = x_frame[part, :].astype(jnp.float32) + dot(mix_frame[part, :], wo0[...])
+        def arrive(k, c):
+            source = partner_at(k)
+            m_copy(source, source).wait_recv()
+            return c
+
+        lax.fori_loop(jnp.maximum(i * per_block, 1), (i + 1) * per_block, arrive, 0)
+        b = partner_at(i * per_block) // per_block
+        f_copy(b, s).start()
+        f_copy(b, 1 - s).wait_recv()
+        part = rows(b, BLOCK)
+        halves = [
+            mix_frame[rows(core * blocks + b, gathered), :].reshape(per_block, 1, half, INNER)
+            for core in range(2)
+        ]
+        mixed = jnp.concatenate(halves, axis=1).reshape(BLOCK, INNER)
+        grown = x_frame[part, :].astype(jnp.float32) + dot(mixed, wo0[...])
         grown = grown.astype(jnp.bfloat16)
         first1[part, :] = grown
         qkv1[part, :] = dot(normalize(grown), wq1[...]).astype(jnp.bfloat16)
         return c
 
-    lax.fori_loop(0, tracks // 256, middle, 0)
+    lax.fori_loop(0, blocks, middle, 0)
 
     r = lax.broadcasted_iota(jnp.int32, (BLOCK, tracks), 0)
     t = lax.broadcasted_iota(jnp.int32, (BLOCK, tracks), 1)
     track = lax.broadcasted_iota(jnp.int32, (1, tracks), 1)
     block_of = track // BLOCK
+    near_at = lax.broadcasted_iota(jnp.int32, (NB, blocks), 1)
     seen = seen_ref[...] == 1
 
     def low_copy(b):
@@ -434,7 +444,8 @@
 
     def attend(b, c):
         part = rows(b, BLOCK)
-        listed = (block_of == b) | (block_of == near_ref[b, 0]) | (block_of == near_ref[b, 1])
+        near = jnp.sum(jnp.where(near_at == b, near_ref[...], 0), axis=1, keepdims=True)
+        listed = (block_of == b) | (block_of == near[0:1]) | (block_of == near[1:2])
         open_row = jnp.where(seen & listed, 1.0, 0.0)
         allow = jnp.where(t == r + b * BLOCK, 1.0, open_row) > 0.5
         for h in range(HALF_HEADS):
@@ -452,12 +463,6 @@
         return c
 
     lax.fori_loop(0, blocks, attend, 0)
-    per_block = BLOCK // group
-
-    def out_copy(b):
-        return pltpu.make_async_copy(
-            second.at[rows(b, per_block)], out_ref.at[rows(b, per_block)], out_sem.at[1 + b]
-        )
 
     @pl.when(s == 1)
     def _():
@@ -466,28 +471,20 @@
         def close(b, c):
             part = rows(b, BLOCK)
             low_copy(b).wait_recv()
-            delta = dot(mix1_low[part, :], wo1[:HALF_INNER, :]) + dot(
-                mix1[part, :], wo1[HALF_INNER:, :]
+            mixed = jnp.concatenate([mix1_low[part, :], mix1[part, :]], axis=1)
+            total = first1[part, :].astype(jnp.float32) + dot(mixed, wo1[...])
+            out_ref[rows(b, per_block)] = total.astype(jnp.bfloat16).reshape(
+                per_block, 2, half, -1
             )
-            total = (first1[part, :].astype(jnp.float32) + delta).astype(jnp.bfloat16)
-            second[rows(b, per_block)] = total.reshape(per_block, 2, half, -1)
-            out_copy(b).start()
             return c
 
         lax.fori_loop(0, blocks, close, 0)
-
-        def closed(b, c):
-            out_copy(b).wait()
-            return c
-
-        lax.fori_loop(0, blocks, closed, 0)
         out_remote.wait_send()
         for copy in wq1_remote:
             copy.wait_send()
 
     @pl.when(s == 0)
     def _():
-        out_first.wait()
         out_remote.wait_recv()
         wq0_remote.wait_send()
         wo0_remote.wait_send()
@@ -499,14 +496,18 @@
         lax.fori_loop(0, blocks, sent_low, 0)
 
     def drain(k, c):
-        d = lax.rem(me + k, n)
+        d = partner_at(k)
         x_copy(d, me).wait_send()
         m_copy(d, me).wait_send()
-        f_copy(d, s).wait_send()
         return c
 
     lax.fori_loop(1, n, drain, 0)
-    f_copy(me, s).wait_send()
+
+    def drain_forwards(b, c):
+        f_copy(b, s).wait_send()
+        return c
+
+    lax.fori_loop(0, blocks, drain_forwards, 0)
 
 
 def on_device_fused(tracks_in, w_qkv, w_out, visible, neighbours):
@@ -517,13 +518,13 @@
     blocks = tracks // BLOCK
     bf16 = jnp.bfloat16
     dma = pltpu.SemaphoreType.DMA
-    anywhere = pl.BlockSpec(memory_space=pl.ANY)
+    in_hbm = pl.BlockSpec(memory_space=pltpu.HBM)
     out = pl.pallas_call(
         functools.partial(fused_kernel, n, half),
         out_shape=jax.ShapeDtypeStruct((n, 2, half, width), bf16),
-        in_specs=[anywhere] * 3
-        + [pl.BlockSpec(memory_space=pltpu.VMEM), pl.BlockSpec(memory_space=pltpu.SMEM)],
-        out_specs=anywhere,
+        in_specs=[in_hbm] * 3
+        + [pl.BlockSpec(memory_space=pltpu.VMEM)] * 2,
+        out_specs=pl.BlockSpec(memory_space=pltpu.VMEM),
         scratch_shapes=[
             pltpu.VMEM((width, 3 * INNER), bf16),
             pltpu.VMEM((INNER, width), bf16),
@@ -540,7 +541,6 @@
             pltpu.VMEM((tracks, 3 * HALF_INNER), bf16),
             pltpu.VMEM((tracks, HALF_INNER), bf16),
             pltpu.VMEM((tracks, HALF_INNER), bf16),
-            pltpu.VMEM((n, 2, half, width), bf16),
             dma((6,)),
             dma((5,)),
             dma((n,)),
@@ -548,16 +548,15 @@
             dma,
             dma((n,)),
             dma((n,)),
-            dma((n,)),
-            dma((n,)),
             dma((blocks,)),
             dma((blocks,)),
-            dma((1 + blocks,)),
+            dma((blocks,)),
+            dma((blocks,)),
             dma,
             dma,
         ],
         compiler_params=pltpu.CompilerParams(
-            collective_id=0, has_side_effects=True, vmem_limit_bytes=56 * 1024 * 1024
+            collective_id=0, has_side_effects=True, vmem_limit_bytes=32 * 1024 * 1024
         ),
         cost_estimate=pl.CostEstimate(
             flops=9_000_000_000, bytes_accessed=20_000_000, transcendentals=1_200_000
@@ -567,7 +566,7 @@
         w_qkv.reshape(width, 3 * INNER),
         w_out.reshape(INNER, width),
         visible.reshape(1, tracks),
-        neighbours.reshape(blocks, NB),
+        neighbours.reshape(blocks, NB).T,
     )
     return out.reshape(1, 1, 1, tracks, width)
 

time: 54.4 us -> 57.7 us (1.061)
  local copies, waits for them, and re-layouts: 3.99 us -> 8.58 us
  Pallas kernels: 49.8 us -> 48.9 us
    unnamed x1 -> x11, local copies, waits for them, and re-layouts: 2.65 us -> 8.58 us
    reshape x1 -> x0, local copies, waits for them, and re-layouts: 1.34 us -> none  [on_device_fused(): neighbours.reshape(blocks, NB)]
    pallas_call x1, Pallas kernels: 49.8 us -> 48.9 us  [on_device_fused(): pl.pallas_call(functools.partial(fused_kernel, n, half), out_shape=jax.Sh...]
where the time goes in v3:
time: 57.7 us; the launch traced here: 57.5 us
  Pallas kernels  48.9 us (85%)
  local copies, waits for them, and re-layouts  8.58 us (15%)
    pallas_call x1, Pallas kernels, on_device_fused(): pl.pallas_call(functools.partial(fused_kernel, n, half), out_shape=jax.Sh...  48.9 us
    unnamed x11, local copies, waits for them, and re-layouts  8.58 us

profile of v3, /device:TPU:9, one launch (start us, length us, event | category | flops | bytes accessed | tf_op | source)
XLA Modules:
  0.0 57.5 jit_solution(16868729724891078029)
XLA Ops:
  0.0 0.0 copy-start
  0.0 3.0 %copy-done = bf16[1,1536,2304]{2,1,0:T(8,128)(2,1)S(1)} copy-done((bf16[1,1536,2304]{2,1,0:T(8,128)(2,1)S(1)}, bf16[1,1536,2304]{2,1,0:T(8,128)(2,1)}, u32[]{:S(2)}) %copy-start) | copy-done | bytes 7077912
  3.0 0.0 copy-start.1
  3.0 1.7 %copy-done.1 = bf16[1,768,1536]{2,1,0:T(8,128)(2,1)S(1)} copy-done((bf16[1,768,1536]{2,1,0:T(8,128)(2,1)S(1)}, bf16[1,768,1536]{2,1,0:T(8,128)(2,1)}, u32[]{:S(2)}) %copy-start.1) | copy-done | bytes 2359320
  4.7 0.0 copy-start.2
  4.7 1.4 %copy-done.2 = bf16[1,1,512,1536]{3,2,1,0:T(8,128)(2,1)S(1)} copy-done((bf16[1,1,512,1536]{3,2,1,0:T(8,128)(2,1)S(1)}, bf16[1,1,512,1536]{3,2,1,0:T(8,128)(2,1)}, u32[]{:S(2)}) %copy-start.2) | copy-done | bytes 1572888
  6.1 0.0 copy-start.3
  6.1 0.7 %copy-done.3 = s32[1,1,512]{2,1,0:T(1,128)S(1)} copy-done((s32[1,1,512]{2,1,0:T(1,128)S(1)}, s32[1,1,512]{2,1,0:T(1,128)}, u32[]{:S(2)}) %copy-start.3) | copy-done | bytes 2072
  6.8 0.0 copy-start.4
  6.8 0.7 %copy-done.4 = s32[1,1,4,2]{2,3,1,0:T(2,128)S(1)} copy-done((s32[1,1,4,2]{2,3,1,0:T(2,128)S(1)}, s32[1,1,4,2]{2,3,1,0:T(2,128)}, u32[]{:S(2)}) %copy-start.4) | copy-done | bytes 56
  7.4 48.9 %shard_map.55 = bf16[16,2,16,1536]{3,2,1,0:T(8,128)(2,1)S(1)} custom-call(bf16[512,1536]{1,0:T(8,128)(2,1)S(1)} %bitcast.11, bf16[1536,2304]{1,0:T(8,128)(2,1)S(1)} %bitcast.9, bf16[768,1536]{1,0:T(8,128)(2,1)S(1)} %bitcast.10, s32[1,512]{1,0:T(1,128)S(1)} %bitcast.12, s32[2,4]{1,0:T(2,128)S(1)} %bitcast.13), custom_call_target="tpu_custom_call" | custom-call | flops 8999999488 | bytes 20000000 | tf_op jit(solution)/shard_map/pallas_call | solution.py:522
  56.3 1.1 %copy.7 = bf16[1,1,1,512,1536]{4,3,2,1,0:T(8,128)(2,1)} copy(bf16[1,1,1,512,1536]{4,3,2,1,0:T(8,128)(2,1)S(1)} %bitcast.8) | data formatting | bytes 3145728
Async XLA Ops:
  0.0 3.0 %copy-start = (bf16[1,1536,2304]{2,1,0:T(8,128)(2,1)S(1)}, bf16[1,1536,2304]{2,1,0:T(8,128)(2,1)}, u32[]{:S(2)}) copy-start(bf16[1,1536,2304]{2,1,0:T(8,128)(2,1)} %param.6) | copy-start | bytes 21233668
  3.0 1.7 %copy-start.1 = (bf16[1,768,1536]{2,1,0:T(8,128)(2,1)S(1)}, bf16[1,768,1536]{2,1,0:T(8,128)(2,1)}, u32[]{:S(2)}) copy-start(bf16[1,768,1536]{2,1,0:T(8,128)(2,1)} %param.7) | copy-start | bytes 7077892
  4.7 1.4 %copy-start.2 = (bf16[1,1,512,1536]{3,2,1,0:T(8,128)(2,1)S(1)}, bf16[1,1,512,1536]{3,2,1,0:T(8,128)(2,1)}, u32[]{:S(2)}) copy-start(bf16[1,1,512,1536]{3,2,1,0:T(8,128)(2,1)} %param.5) | copy-start | bytes 4718596
  6.1 0.7 %copy-start.3 = (s32[1,1,512]{2,1,0:T(1,128)S(1)}, s32[1,1,512]{2,1,0:T(1,128)}, u32[]{:S(2)}) copy-start(s32[1,1,512]{2,1,0:T(1,128)} %param.8) | copy-start | bytes 6148
  6.8 0.7 %copy-start.4 = (s32[1,1,4,2]{2,3,1,0:T(2,128)S(1)}, s32[1,1,4,2]{2,3,1,0:T(2,128)}, u32[]{:S(2)}) copy-start(s32[1,1,4,2]{2,3,1,0:T(2,128)} %param.9) | copy-start | bytes 100

commit v4 on v3

--- a/solution.py
+++ b/solution.py
@@ -139,6 +139,7 @@
 HALF_HEADS = HEADS // 2
 HALF_INNER = HALF_HEADS * HDIM
 MESH = pl.DeviceIdType.MESH
+MASKED = -1e30
 SCALE_LOG2 = math.log2(math.e) / math.sqrt(HDIM)
 
 
@@ -174,6 +175,8 @@
     qkv1,
     mix1,
     mix1_low,
+    bias0,
+    bias1,
     w_sem,
     w_send,
     x_send,
@@ -294,6 +297,20 @@
 
     frame_copy.start()
 
+    i0 = lax.broadcasted_iota(jnp.int32, (tokens, tokens), 0)
+    i1 = lax.broadcasted_iota(jnp.int32, (tokens, tokens), 1)
+    bias0[...] = jnp.where(lax.rem(i0, half) == lax.rem(i1, half), 0.0, MASKED)
+    r = lax.broadcasted_iota(jnp.int32, (BLOCK, tracks), 0)
+    t = lax.broadcasted_iota(jnp.int32, (BLOCK, tracks), 1)
+    block_of = lax.broadcasted_iota(jnp.int32, (1, tracks), 1) // BLOCK
+    seen = seen_ref[...] == 1
+    for b in range(blocks):
+        listed = block_of == b
+        for j in range(NB):
+            listed = listed | (block_of == near_ref[j : j + 1, b : b + 1])
+        open_row = jnp.where(seen & listed, 0.0, MASKED)
+        bias1[b * BLOCK : (b + 1) * BLOCK, :] = jnp.where(t == r + b * BLOCK, 0.0, open_row)
+
     def norm_rows(k, c):
         source = partner_at(k)
 
@@ -325,14 +342,11 @@
 
     lax.fori_loop(0, 2, project0, 0)
 
-    i0 = lax.broadcasted_iota(jnp.int32, (tokens, tokens), 0)
-    i1 = lax.broadcasted_iota(jnp.int32, (tokens, tokens), 1)
-    same = lax.rem(i0, half) == lax.rem(i1, half)
     for h in range(HEADS):
         q = qkv0[:, h * HDIM : (h + 1) * HDIM]
         k = qkv0[:, INNER + h * HDIM : INNER + (h + 1) * HDIM]
         v = qkv0[:, 2 * INNER + h * HDIM : 2 * INNER + (h + 1) * HDIM]
-        e = jnp.where(same, jnp.exp2(dot_t(q, k) * SCALE_LOG2), 0.0)
+        e = jnp.exp2(dot_t(q, k) * SCALE_LOG2 + bias0[...])
         w = (e * (1.0 / jnp.sum(e, axis=-1, keepdims=True))).astype(jnp.bfloat16)
         mix0[:, h * HDIM : (h + 1) * HDIM] = dot(w, v).astype(jnp.bfloat16)
 
@@ -425,60 +439,44 @@
 
     lax.fori_loop(0, blocks, middle, 0)
 
-    r = lax.broadcasted_iota(jnp.int32, (BLOCK, tracks), 0)
-    t = lax.broadcasted_iota(jnp.int32, (BLOCK, tracks), 1)
-    track = lax.broadcasted_iota(jnp.int32, (1, tracks), 1)
-    block_of = track // BLOCK
-    near_at = lax.broadcasted_iota(jnp.int32, (NB, blocks), 1)
-    seen = seen_ref[...] == 1
-
-    def low_copy(b):
+    span = tracks // 2
+
+    def low_copy(i):
+        place = pl.ds(i * span, span)
         return pltpu.make_async_remote_copy(
-            src_ref=mix1.at[rows(b, BLOCK), :],
-            dst_ref=mix1_low.at[rows(b, BLOCK), :],
-            send_sem=low_send.at[b],
-            recv_sem=low_recv.at[b],
+            src_ref=mix1.at[place, :],
+            dst_ref=mix1_low.at[place, :],
+            send_sem=low_send.at[i],
+            recv_sem=low_recv.at[i],
             device_id=sibling,
             device_id_type=MESH,
         )
 
-    def attend(b, c):
-        part = rows(b, BLOCK)
-        near = jnp.sum(jnp.where(near_at == b, near_ref[...], 0), axis=1, keepdims=True)
-        listed = (block_of == b) | (block_of == near[0:1]) | (block_of == near[1:2])
-        open_row = jnp.where(seen & listed, 1.0, 0.0)
-        allow = jnp.where(t == r + b * BLOCK, 1.0, open_row) > 0.5
+    for i in range(2):
+        part = slice(i * span, (i + 1) * span)
         for h in range(HALF_HEADS):
             q = qkv1[part, h * HDIM : (h + 1) * HDIM]
             k = qkv1[:, HALF_INNER + h * HDIM : HALF_INNER + (h + 1) * HDIM]
             v = qkv1[:, 2 * HALF_INNER + h * HDIM : 2 * HALF_INNER + (h + 1) * HDIM]
-            e = jnp.where(allow, jnp.exp2(dot_t(q, k) * SCALE_LOG2), 0.0)
+            e = jnp.exp2(dot_t(q, k) * SCALE_LOG2 + bias1[part, :])
             w = (e * (1.0 / jnp.sum(e, axis=-1, keepdims=True))).astype(jnp.bfloat16)
             mix1[part, h * HDIM : (h + 1) * HDIM] = dot(w, v).astype(jnp.bfloat16)
 
         @pl.when(s == 0)
         def _():
-            low_copy(b).start()
-
-        return c
-
-    lax.fori_loop(0, blocks, attend, 0)
+            low_copy(i).start()
 
     @pl.when(s == 1)
     def _():
         wo1_local.wait()
-
-        def close(b, c):
-            part = rows(b, BLOCK)
-            low_copy(b).wait_recv()
+        for i in range(2):
+            part = slice(i * span, (i + 1) * span)
+            low_copy(i).wait_recv()
             mixed = jnp.concatenate([mix1_low[part, :], mix1[part, :]], axis=1)
             total = first1[part, :].astype(jnp.float32) + dot(mixed, wo1[...])
-            out_ref[rows(b, per_block)] = total.astype(jnp.bfloat16).reshape(
-                per_block, 2, half, -1
+            out_ref[i * n // 2 : (i + 1) * n // 2] = total.astype(jnp.bfloat16).reshape(
+                n // 2, 2, half, -1
             )
-            return c
-
-        lax.fori_loop(0, blocks, close, 0)
         out_remote.wait_send()
         for copy in wq1_remote:
             copy.wait_send()
@@ -489,11 +487,8 @@
         wq0_remote.wait_send()
         wo0_remote.wait_send()
 
-        def sent_low(b, c):
-            low_copy(b).wait_send()
-            return c
-
-        lax.fori_loop(0, blocks, sent_low, 0)
+        for i in range(2):
+            low_copy(i).wait_send()
 
     def drain(k, c):
         d = partner_at(k)
@@ -541,6 +536,8 @@
             pltpu.VMEM((tracks, 3 * HALF_INNER), bf16),
             pltpu.VMEM((tracks, HALF_INNER), bf16),
             pltpu.VMEM((tracks, HALF_INNER), bf16),
+            pltpu.VMEM((tokens, tokens), jnp.float32),
+            pltpu.VMEM((tracks, tracks), jnp.float32),
             dma((6,)),
             dma((5,)),
             dma((n,)),
@@ -556,7 +553,7 @@
             dma,
         ],
         compiler_params=pltpu.CompilerParams(
-            collective_id=0, has_side_effects=True, vmem_limit_bytes=32 * 1024 * 1024
+            collective_id=0, has_side_effects=True, vmem_limit_bytes=52 * 1024 * 1024
         ),
         cost_estimate=pl.CostEstimate(
             flops=9_000_000_000, bytes_accessed=20_000_000, transcendentals=1_200_000

time: 57.7 us -> 49.6 us (0.86)
  local copies, waits for them, and re-layouts: 8.58 us -> 2.5 us
  Pallas kernels: 48.9 us -> 47 us
    unnamed x11 -> x5, local copies, waits for them, and re-layouts: 8.58 us -> 2.5 us
    pallas_call x1, Pallas kernels: 48.9 us -> 47 us  [on_device_fused(): pl.pallas_call(functools.partial(fused_kernel, n, half), out_shape=jax.Sh...]
where the time goes in v4:
time: 49.6 us; the launch traced here: 49.5 us
  Pallas kernels  47 us (95%)
  local copies, waits for them, and re-layouts  2.5 us (5%)
    pallas_call x1, Pallas kernels, on_device_fused(): pl.pallas_call(functools.partial(fused_kernel, n, half), out_shape=jax.Sh...  47 us
    unnamed x5, local copies, waits for them, and re-layouts  2.5 us

profile of v4, /device:TPU:9, one launch (start us, length us, event | category | flops | bytes accessed | tf_op | source)
XLA Modules:
  0.0 49.5 jit_solution(17076017339130913802)
XLA Ops:
  0.0 0.0 copy-start
  0.0 0.7 %copy-done = s32[1,1,512]{2,1,0:T(1,128)S(1)} copy-done((s32[1,1,512]{2,1,0:T(1,128)S(1)}, s32[1,1,512]{2,1,0:T(1,128)}, u32[]{:S(2)}) %copy-start) | copy-done | bytes 2072
  0.7 0.0 copy-start.1
  0.7 0.7 %copy-done.1 = s32[1,1,4,2]{2,3,1,0:T(2,128)S(1)} copy-done((s32[1,1,4,2]{2,3,1,0:T(2,128)S(1)}, s32[1,1,4,2]{2,3,1,0:T(2,128)}, u32[]{:S(2)}) %copy-start.1) | copy-done | bytes 56
  1.4 47.0 %shard_map.55 = bf16[16,2,16,1536]{3,2,1,0:T(8,128)(2,1)S(1)} custom-call(bf16[512,1536]{1,0:T(8,128)(2,1)} %bitcast.13, bf16[1536,2304]{1,0:T(8,128)(2,1)} %bitcast.11, bf16[768,1536]{1,0:T(8,128)(2,1)} %bitcast.12, s32[1,512]{1,0:T(1,128)S(1)} %bitcast.9, s32[2,4]{1,0:T(2,128)S(1)} %bitcast.10), custom_call_target="tpu_custom_call" | custom-call | flops 8999999488 | bytes 20000000 | tf_op jit(solution)/shard_map/pallas_call | solution.py:517
  48.3 1.1 %copy.7 = bf16[1,1,1,512,1536]{4,3,2,1,0:T(8,128)(2,1)} copy(bf16[1,1,1,512,1536]{4,3,2,1,0:T(8,128)(2,1)S(1)} %bitcast.8) | data formatting | bytes 3145728
Async XLA Ops:
  0.0 0.7 %copy-start = (s32[1,1,512]{2,1,0:T(1,128)S(1)}, s32[1,1,512]{2,1,0:T(1,128)}, u32[]{:S(2)}) copy-start(s32[1,1,512]{2,1,0:T(1,128)} %param.8) | copy-start | bytes 6148
  0.7 0.7 %copy-start.1 = (s32[1,1,4,2]{2,3,1,0:T(2,128)S(1)}, s32[1,1,4,2]{2,3,1,0:T(2,128)}, u32[]{:S(2)}) copy-start(s32[1,1,4,2]{2,3,1,0:T(2,128)} %param.9) | copy-start | bytes 100

commit v5 on v4

--- a/solution.py
+++ b/solution.py
@@ -402,7 +402,6 @@
     @pl.when(s == 1)
     def _():
         first0[...] = added
-        out_remote.start()
 
     frame_copy.wait()
     for j in range(3):
@@ -438,6 +437,10 @@
         return c
 
     lax.fori_loop(0, blocks, middle, 0)
+
+    @pl.when(s == 1)
+    def _():
+        out_remote.start()
 
     span = tracks // 2
 

time: 49.6 us -> 49.7 us (level)
  no operation moved by 1% of the time
where the time goes in v5:
time: 49.7 us; the launch traced here: 49.5 us
  Pallas kernels  47 us (95%)
  local copies, waits for them, and re-layouts  2.5 us (5%)
    pallas_call x1, Pallas kernels, on_device_fused(): pl.pallas_call(functools.partial(fused_kernel, n, half), out_shape=jax.Sh...  47 us
    unnamed x5, local copies, waits for them, and re-layouts  2.5 us

profile of v5, /device:TPU:9, one launch (start us, length us, event | category | flops | bytes accessed | tf_op | source)
XLA Modules:
  0.0 49.5 jit_solution(9248471008263863698)
XLA Ops:
  0.0 0.0 copy-start
  0.0 0.7 %copy-done = s32[1,1,512]{2,1,0:T(1,128)S(1)} copy-done((s32[1,1,512]{2,1,0:T(1,128)S(1)}, s32[1,1,512]{2,1,0:T(1,128)}, u32[]{:S(2)}) %copy-start) | copy-done | bytes 2072
  0.7 0.0 copy-start.1
  0.7 0.7 %copy-done.1 = s32[1,1,4,2]{2,3,1,0:T(2,128)S(1)} copy-done((s32[1,1,4,2]{2,3,1,0:T(2,128)S(1)}, s32[1,1,4,2]{2,3,1,0:T(2,128)}, u32[]{:S(2)}) %copy-start.1) | copy-done | bytes 56
  1.4 47.0 %shard_map.55 = bf16[16,2,16,1536]{3,2,1,0:T(8,128)(2,1)S(1)} custom-call(bf16[512,1536]{1,0:T(8,128)(2,1)} %bitcast.13, bf16[1536,2304]{1,0:T(8,128)(2,1)} %bitcast.11, bf16[768,1536]{1,0:T(8,128)(2,1)} %bitcast.12, s32[1,512]{1,0:T(1,128)S(1)} %bitcast.9, s32[2,4]{1,0:T(2,128)S(1)} %bitcast.10), custom_call_target="tpu_custom_call" | custom-call | flops 8999999488 | bytes 20000000 | tf_op jit(solution)/shard_map/pallas_call | solution.py:520
  48.3 1.1 %copy.7 = bf16[1,1,1,512,1536]{4,3,2,1,0:T(8,128)(2,1)} copy(bf16[1,1,1,512,1536]{4,3,2,1,0:T(8,128)(2,1)S(1)} %bitcast.8) | data formatting | bytes 3145728
Async XLA Ops:
  0.0 0.7 %copy-start = (s32[1,1,512]{2,1,0:T(1,128)S(1)}, s32[1,1,512]{2,1,0:T(1,128)}, u32[]{:S(2)}) copy-start(s32[1,1,512]{2,1,0:T(1,128)} %param.8) | copy-start | bytes 6148
  0.7 0.7 %copy-start.1 = (s32[1,1,4,2]{2,3,1,0:T(2,128)S(1)}, s32[1,1,4,2]{2,3,1,0:T(2,128)}, u32[]{:S(2)}) copy-start(s32[1,1,4,2]{2,3,1,0:T(2,128)} %param.9) | copy-start | bytes 100
